TPU v7x, 32 devices: a whole 2x2x4 slice. The times are simulated.
32 devices in a mesh: groups: 2 (over x), ctx: 4 (over y, core), head: 4 (over z).
Axes of the slice: x: 2, y: 2, z: 4, core: 2. Of those that a mesh axis runs over, the one named last changes fastest.
Arguments:
- queries: bfloat16 [256, 16384], P(('groups', 'ctx'), 'head'), parts along dimension 0, may hold values from -8 to 8
- cache_keys: bfloat16 [16384, 1024], P(('groups', 'ctx'), 'head'), parts along dimension 0, may hold values from -6 to 6
- cache_values: bfloat16 [16384, 1024], P(('groups', 'ctx'), 'head'), parts along dimension 0, may hold values from -6 to 6
- new_keys: bfloat16 [256, 1024], P(('groups', 'ctx'), 'head'), parts along dimension 0, may hold values from -8 to 8
- new_values: bfloat16 [256, 1024], P(('groups', 'ctx'), 'head'), parts along dimension 0, may hold values from -6 to 6
- out_weight: bfloat16 [16384, 16384], P('head', 'ctx'), may hold values from -0.1796875 to 0.1796875
- new_counts: int32 [8, 4], P('groups'), parts along dimension 0, may hold values from 1 to 16, 32 in all within a row
- cache_counts: int32 [8, 4], P('groups'), parts along dimension 0, may hold values from 1 to 512, 1536 in all within a row
- row_dest: int32 [256], P('groups'), parts along dimension 0, may hold values from 0 to 127, each once
Outputs:
- projected: bfloat16 [256, 16384], P(('groups', 'head'), 'ctx'), parts along dimension 0
There are 2 independent parts, one for each index of `groups`. A program takes and returns all parts, laid end to end along the dimension named above; an argument that names none is the same for every part. Nothing has to cross between parts.
Inputs may be any that keep to these rules, and one draw needn't show every extreme that they name: Each row of new_counts sums to 32. `cache_counts`: each shard's counts sum to 1536. `row_dest`: each output row is named once.
All inputs are finite; a program needn't handle non-finite values.
Results may differ from a plain program's by a relative error of at most 0.017.
Values may be sent and summed in bfloat16 or wider, within the bound.
No kernel may reach another device: no remote copies, remote signals or barrier semaphores. Data moves between devices by JAX's collectives and lax.ppermute only.
A program may use at most 128 MiB of HBM per device.

v0:
```python
import functools
import math

import jax
import jax.numpy as jnp
from jax import lax
from jax.experimental import pallas as pl
from jax.experimental.pallas import tpu as pltpu
from jax.sharding import PartitionSpec as P

HEAD_DIM = 128
CAPR = 512
ROWS = 16
ALIGN = 16
NEG = -1e30
SCALE = 1.0 / math.sqrt(HEAD_DIM)
LOG2E = math.log2(math.e)


def in_hbm(a):
    return pltpu.with_memory_space_constraint(a, pltpu.HBM)


def pack_kernel(number, kv, index, *refs):
    sources, out_ref, sems = refs[:-2], refs[-2], refs[-1]
    block = index[0] * kv + number
    copies = []
    at = 0
    for ref in sources[:4]:
        rows = ref.shape[0]
        columns = pl.ds(pl.multiple_of(block * HEAD_DIM, HEAD_DIM), HEAD_DIM)
        copies.append((ref.at[:, columns], out_ref.at[at : at + rows, :]))
        at += rows
    for ref in sources[4:]:
        rows = ref.shape[0]
        heads = (out_ref.shape[0] - at) // rows
        for g in range(heads):
            columns = pl.ds(pl.multiple_of((block * heads + g) * HEAD_DIM, HEAD_DIM), HEAD_DIM)
            copies.append((ref.at[:, columns], out_ref.at[at : at + rows, :]))
            at += rows
    copies = [pltpu.make_async_copy(a, b, sems.at[n]) for n, (a, b) in enumerate(copies)]
    for c in copies:
        c.start()
    for c in copies:
        c.wait()


def pack(index, arrays, queries, kv, number):
    group = queries[0].shape[1] // arrays[0].shape[1] if queries else 0
    rows = sum(a.shape[0] for a in arrays) + sum(q.shape[0] * group for q in queries)
    return pl.pallas_call(
        functools.partial(pack_kernel, number, kv),
        in_specs=[pl.BlockSpec(memory_space=pltpu.SMEM)]
        + [pl.BlockSpec(memory_space=pltpu.HBM)] * (len(arrays) + len(queries)),
        out_specs=pl.BlockSpec(memory_space=pltpu.VMEM),
        out_shape=jax.ShapeDtypeStruct((rows, HEAD_DIM), arrays[0].dtype),
        scratch_shapes=[pltpu.SemaphoreType.DMA((len(arrays) + group,))],
        compiler_params=pltpu.CompilerParams(vmem_limit_bytes=4 * 2**20),
        name="pack",
    )(index.reshape(1), *[in_hbm(a) for a in (*arrays, *queries)])


def split_kernel(index, q_ref, *refs):
    outs, sems = refs[:-1], refs[-1]
    width = outs[0].shape[1]
    copies = []
    for n, out in enumerate(outs):
        columns = pl.ds(pl.multiple_of((index[0] ^ n) * width, width), width)
        copies.append(pltpu.make_async_copy(q_ref.at[:, columns], out, sems.at[n]))
    for c in copies:
        c.start()
    for c in copies:
        c.wait()


def split(index, a):
    half = jax.ShapeDtypeStruct((a.shape[0], a.shape[1] // 2), a.dtype)
    return pl.pallas_call(
        split_kernel,
        in_specs=[pl.BlockSpec(memory_space=pltpu.SMEM), pl.BlockSpec(memory_space=pltpu.HBM)],
        out_specs=[pl.BlockSpec(memory_space=pltpu.VMEM)] * 2,
        out_shape=[half, half],
        scratch_shapes=[pltpu.SemaphoreType.DMA((2,))],
        compiler_params=pltpu.CompilerParams(vmem_limit_bytes=2 * 2**20),
        name="split",
    )(index.reshape(1), in_hbm(a))


def attention_kernel(
    blocks, sets, query_blocks, reqs, window, shard_rows, block_rows, near_queries,
    numbers, *rest,
):
    packed = rest[:sets]
    q_refs = rest[sets:-5]
    out_ref, stat_ref, sorted_q, part, stat = rest[-5:]
    shards = sets
    padded = sorted_q.shape[0]
    cols = sorted_q.shape[1]
    group = cols // HEAD_DIM
    all_rows = out_ref.shape[0]
    base_new = sets + query_blocks
    base_cache = base_new + blocks * reqs

    def new_counts(b, r):
        return numbers[base_new + b * reqs + r]

    def cache_counts(b, r):
        return numbers[base_cache + b * reqs + r]

    row_blocks = [numbers[sets + b] for b in range(query_blocks)]
    starts = [[jnp.int32(0)] for _ in row_blocks]
    bases = [[] for _ in row_blocks]
    tile_ends = []
    last = jnp.int32(0)
    for r in range(reqs):
        amount = jnp.int32(0)
        for b, block in enumerate(row_blocks):
            bases[b].append(amount)
            amount = amount + new_counts(block, r)
            starts[b].append(starts[b][-1] + new_counts(block, r))
        last = last + (amount + (ROWS - 1)) // ROWS
        tile_ends.append(last)
    tile_starts = [jnp.int32(0)] + tile_ends[:-1]

    offset = lax.broadcasted_iota(jnp.int32, (1, all_rows), 1)
    pos = jnp.zeros((1, all_rows), jnp.int32)
    for b in range(query_blocks):
        here = offset - b * block_rows
        for r in range(reqs):
            mine = (here >= starts[b][r]) & (here < starts[b][r + 1])
            mine = mine & (here >= 0) & (here < block_rows)
            first = tile_starts[r] * ROWS + bases[b][r] - starts[b][r]
            pos = jnp.where(mine, first + here, pos)
    sorter = (lax.broadcasted_iota(jnp.int32, (padded, all_rows), 0) == pos).astype(jnp.bfloat16)
    rows_in = [q[...] for q in q_refs]
    if near_queries:
        first = 2 * (shard_rows + block_rows)
        near = [
            packed[1][first + g * block_rows : first + (g + 1) * block_rows, :]
            for g in range(group)
        ]
        rows_in.insert(1, jnp.concatenate(near, axis=1))
    rows_in = jnp.concatenate(rows_in, axis=0)
    sorted_q[...] = jnp.dot(sorter, rows_in, preferred_element_type=jnp.float32).astype(
        jnp.bfloat16
    )
    part[...] = jnp.zeros_like(part)
    stat[...] = jnp.zeros_like(stat)

    width = shards * (window + block_rows)
    plain = (shards * window) // 128 * 128
    key = lax.broadcasted_iota(jnp.int32, (1, width), 1)
    lane = lax.broadcasted_iota(jnp.int32, (ROWS, 128), 1)
    ones = jnp.ones((width, HEAD_DIM), jnp.bfloat16)

    def tile(i, carry):
        r = jnp.int32(0)
        start_tile = jnp.int32(0)
        for e in tile_ends[:-1]:
            r = r + (i >= e).astype(jnp.int32)
            start_tile = jnp.where(i >= e, e, start_tile)
        inside = None
        key_pos = jnp.full((1, width), -1, jnp.int32)
        ks, vs = [], []
        for j in range(shards):
            shard = numbers[j]
            low = jnp.int32(0)
            new_low = jnp.int32(0)
            for o in range(reqs - 1):
                low = low + jnp.where(o < r, cache_counts(shard, o), 0)
                new_low = new_low + jnp.where(o < r, new_counts(shard, o), 0)
            high = low + cache_counts(shard, r)
            new_high = new_low + new_counts(shard, r)
            start = jnp.clip(low // ALIGN * ALIGN, 0, shard_rows - window)
            start = pl.multiple_of(start, ALIGN)
            ks.append(packed[j][pl.ds(start, window), :])
            vs.append(packed[j][pl.ds(pl.multiple_of(start + shard_rows, ALIGN), window), :])
            first = key - j * window + start
            seen = (key >= j * window) & (key < (j + 1) * window)
            seen = seen & (first >= low) & (first < high)
            inside = seen if inside is None else inside | seen
            base = shards * window + j * block_rows
            fresh = key - base
            seen = (key >= base) & (fresh < block_rows)
            key_pos = jnp.where(seen, shard * block_rows + fresh, key_pos)
            inside = inside | (seen & (fresh >= new_low) & (fresh < new_high))
        after = 2 * shard_rows
        for j in range(shards):
            ks.append(packed[j][after : after + block_rows, :])
            vs.append(packed[j][after + block_rows : after + 2 * block_rows, :])
        ks = jnp.concatenate(ks, axis=0)
        vs = jnp.concatenate(vs, axis=0)
        row0 = pl.multiple_of(i * ROWS, ROWS)
        q = jnp.concatenate(
            [
                sorted_q[pl.ds(row0, ROWS), g * HEAD_DIM : (g + 1) * HEAD_DIM]
                for g in range(group)
            ],
            axis=0,
        )
        scores = lax.dot_general(
            q, ks, (((1,), (1,)), ((), ())), preferred_element_type=jnp.float32
        )
        bias = jnp.where(inside, 0.0, NEG)
        t = jnp.zeros((ROWS, 1), jnp.int32)
        among = (i - start_tile) * ROWS + lax.broadcasted_iota(jnp.int32, (ROWS, 1), 0)
        base = jnp.int32(0)
        for block in row_blocks:
            begin = jnp.int32(0)
            for o in range(reqs - 1):
                begin = begin + jnp.where(o < r, new_counts(block, o), 0)
            t = jnp.where(among >= base, block * block_rows + begin + among - base, t)
            base = base + new_counts(block, r)
        causal = jnp.where(key_pos[:, plain:] <= t, bias[:, plain:], NEG)
        causal = jnp.concatenate([causal] * group, axis=0)
        scores = jnp.concatenate(
            [scores[:, :plain] + bias[:, :plain], scores[:, plain:] + causal], axis=1
        )
        top = jnp.max(scores, axis=1, keepdims=True)
        probs = jnp.exp2((scores - top) * (SCALE * LOG2E)).astype(jnp.bfloat16)
        mixed = jnp.dot(
            probs,
            jnp.concatenate([vs, ones], axis=1),
            preferred_element_type=jnp.float32,
        )
        total = mixed[:, HEAD_DIM:]
        value = (mixed[:, :HEAD_DIM] / total).astype(jnp.bfloat16)
        lse = top * SCALE + jnp.log(total)
        logs = jnp.zeros((ROWS, 128), jnp.float32)
        for g in range(group):
            rows = slice(g * ROWS, (g + 1) * ROWS)
            part[pl.ds(row0, ROWS), g * HEAD_DIM : (g + 1) * HEAD_DIM] = value[rows]
            logs = jnp.where(lane == g, lse[rows], logs)
        stat[pl.ds(row0, ROWS), :] = logs
        return carry

    lax.fori_loop(0, last, tile, jnp.int32(0))

    back = (((0,), (0,)), ((), ()))
    out_ref[...] = lax.dot_general(
        sorter, part[...], back, preferred_element_type=jnp.float32
    ).astype(jnp.bfloat16)
    stat_ref[...] = lax.dot_general(
        sorter.astype(jnp.float32),
        stat[...],
        back,
        precision=lax.Precision.HIGHEST,
        preferred_element_type=jnp.float32,
    )


def attend(numbers, packed, queries, cols, number, sizes, query_blocks, near_queries):
    blocks, reqs, shard_rows, block_rows = sizes
    all_rows = query_blocks * block_rows
    padded = (all_rows + reqs * (ROWS - 1)) // ROWS * ROWS
    sets = len(packed)
    window = min(CAPR + ALIGN, shard_rows)
    vmem = pl.BlockSpec(memory_space=pltpu.VMEM)
    return pl.pallas_call(
        functools.partial(
            attention_kernel,
            blocks, sets, query_blocks, reqs, window, shard_rows, block_rows, near_queries,
        ),
        grid_spec=pltpu.PrefetchScalarGridSpec(
            num_scalar_prefetch=1,
            grid=(1,),
            in_specs=[vmem] * sets
            + [pl.BlockSpec((a.shape[0], cols), lambda i, p: (0, number)) for a in queries],
            out_specs=[vmem, vmem],
            scratch_shapes=[
                pltpu.VMEM((padded, cols), jnp.bfloat16),
                pltpu.VMEM((padded, cols), jnp.bfloat16),
                pltpu.VMEM((padded, 128), jnp.float32),
            ],
        ),
        out_shape=[
            jax.ShapeDtypeStruct((all_rows, cols), jnp.bfloat16),
            jax.ShapeDtypeStruct((all_rows, 128), jnp.float32),
        ],
        compiler_params=pltpu.CompilerParams(vmem_limit_bytes=12 * 2**20),
        cost_estimate=pl.CostEstimate(
            flops=8 * padded * cols * sets * window,
            bytes_accessed=16 * 2**20,
            transcendentals=0,
        ),
        name="attend",
    )(numbers, *packed, *queries)


def combine_kernel(group, dest_ref, *refs):
    out_ref = refs[-1]
    rows = out_ref.shape[0]
    landing = (lax.broadcasted_iota(jnp.int32, (rows, rows), 0) == dest_ref[...]).astype(jnp.bfloat16)
    weights = []
    for n in range(0, len(refs) - 1, 4):
        sa, sb = refs[n + 2][...], refs[n + 3][...]
        best = jnp.maximum(sa, sb)
        wa, wb = jnp.exp(sa - best), jnp.exp(sb - best)
        whole = wa + wb
        weights.append((wa / whole, wb / whole))
    for g in range(group):
        at = slice(g * HEAD_DIM, (g + 1) * HEAD_DIM)
        mixed = []
        for n, (wa, wb) in enumerate(weights):
            one = wa[:, g : g + 1] * refs[4 * n][:, at].astype(jnp.float32)
            one = one + wb[:, g : g + 1] * refs[4 * n + 1][:, at].astype(jnp.float32)
            mixed.append(one.astype(jnp.bfloat16))
        mixed = jnp.concatenate(mixed, axis=0)
        out_ref[:, at] = jnp.dot(landing, mixed, preferred_element_type=jnp.float32).astype(jnp.bfloat16)


def combine(dest, phases):
    vmem = pl.BlockSpec(memory_space=pltpu.VMEM)
    arrays = [a for phase in phases for a in phase]
    cols = arrays[0].shape[1]
    return pl.pallas_call(
        functools.partial(combine_kernel, cols // HEAD_DIM),
        in_specs=[vmem] * (1 + len(arrays)),
        out_specs=vmem,
        out_shape=jax.ShapeDtypeStruct((dest.shape[1], cols), jnp.bfloat16),
        compiler_params=pltpu.CompilerParams(vmem_limit_bytes=8 * 2**20),
        name="combine",
    )(dest, *arrays)


def project_kernel(parts, added, cuts, first, step, order, *refs):
    a_refs, w_ref = refs[:parts], refs[parts]
    rest = refs[parts + 1 :]
    total_refs, outs = rest[:added], rest[added : added + len(cuts)]
    held, sems = rest[-2:]
    depth = held.shape[0] // parts
    copies = []
    for j in range(held.shape[1] // step):
        here = slice(j * step, (j + 1) * step)
        for n in range(parts):
            rows = pl.ds(pl.multiple_of(order[n] * depth, ALIGN), depth)
            source = w_ref.at[rows, first + j * step : first + (j + 1) * step]
            target = held.at[n * depth : (n + 1) * depth, here]
            copies.append(pltpu.make_async_copy(source, target, sems.at[len(copies)]))
            copies[-1].start()
    for j in range(held.shape[1] // step):
        here = slice(j * step, (j + 1) * step)
        total = total_refs[0][:, here] if added else None
        for n in range(parts):
            copies[j * parts + n].wait()
            w = held[n * depth : (n + 1) * depth, here]
            product = jnp.dot(a_refs[n][...], w, preferred_element_type=jnp.float32)
            total = product if total is None else total + product
        for (low, high), out in zip(cuts, outs):
            out[:, here] = total[low:high].astype(out.dtype)


def project(order, parts, weight, cuts, first, width, step, added=()):
    vmem = pl.BlockSpec(memory_space=pltpu.VMEM)
    depth = parts[0].shape[1] * len(parts)
    return pl.pallas_call(
        functools.partial(project_kernel, len(parts), len(added), [c[:2] for c in cuts], first, step),
        in_specs=[pl.BlockSpec(memory_space=pltpu.SMEM)]
        + [vmem] * len(parts)
        + [pl.BlockSpec(memory_space=pltpu.HBM)]
        + [vmem] * len(added),
        out_specs=[vmem] * len(cuts),
        out_shape=[jax.ShapeDtypeStruct((high - low, width), dtype) for low, high, dtype in cuts],
        scratch_shapes=[
            pltpu.VMEM((depth, width), weight.dtype),
            pltpu.SemaphoreType.DMA((len(parts) * (width // step),)),
        ],
        compiler_params=pltpu.CompilerParams(vmem_limit_bytes=26 * 2**20),
        cost_estimate=pl.CostEstimate(
            flops=2 * parts[0].shape[0] * depth * width,
            bytes_accessed=2 * depth * width,
            transcendentals=0,
        ),
        name="project",
    )(order, *parts, in_hbm(weight), *added)


def finish_kernel(counts, *refs):
    out_ref = refs[-1]
    at = n = 0
    for count in counts:
        rows, width = refs[n].shape
        total = refs[n][...]
        for ref in refs[n + 1 : n + count]:
            total = total + ref[:rows, :].astype(jnp.float32)
        out_ref[:, at : at + width] = total.astype(out_ref.dtype)
        at += width
        n += count


def finish(chunks):
    vmem = pl.BlockSpec(memory_space=pltpu.VMEM)
    arrays = [a for chunk in chunks for a in chunk]
    width = sum(chunk[0].shape[1] for chunk in chunks)
    return pl.pallas_call(
        functools.partial(finish_kernel, [len(chunk) for chunk in chunks]),
        in_specs=[vmem] * len(arrays),
        out_specs=vmem,
        out_shape=jax.ShapeDtypeStruct((arrays[0].shape[0], width), jnp.bfloat16),
        compiler_params=pltpu.CompilerParams(vmem_limit_bytes=8 * 2**20),
        name="finish",
    )(*arrays)


def per_device(
    queries,
    cache_keys,
    cache_values,
    new_keys,
    new_values,
    out_weight,
    new_counts,
    cache_counts,
    row_dest,
):
    blocks = lax.axis_size("ctx")
    heads = lax.axis_size("head")
    me = lax.axis_index("ctx")
    my_head = lax.axis_index("head")
    block_rows = queries.shape[0]
    all_rows = block_rows * blocks
    reqs = new_counts.shape[1]
    kv_here = cache_keys.shape[1] // HEAD_DIM
    paired = blocks == 4 and kv_here % 2 == 0
    half = me % 2
    even = heads & (heads - 1) == 0
    kv = kv_here // 2 if paired else kv_here
    cols = queries.shape[1] // kv_here
    sizes = (blocks, reqs, cache_keys.shape[0], block_rows)
    caches = (cache_keys, cache_values, new_keys, new_values)

    if paired:
        near = [(i, i ^ 1) for i in range(blocks)]
        far = [(i, i ^ 2) for i in range(blocks)]
        across = [(i, i ^ 3) for i in range(blocks)]
        q_mine, q_other = split(half, queries)
        q_far = lax.ppermute(q_mine, "ctx", far)
        q_across = lax.ppermute(q_other, "ctx", across)
        packed = [
            [
                pack(half, caches, [], kv, i),
                lax.ppermute(pack(1 - half, caches, [queries], kv, i), "ctx", near),
            ]
            for i in range(kv)
        ]
        phases = [([me, me ^ 1], [q_mine]), ([me ^ 2, me ^ 3], [q_far, q_across])]
        key_blocks = [me, me ^ 1]
    else:
        rows_in = lax.all_gather(queries, "ctx", axis=0, tiled=True)
        packed = [
            [jnp.concatenate([a[:, i * HEAD_DIM : (i + 1) * HEAD_DIM] for a in caches], axis=0)]
            for i in range(kv)
        ]
        phases = [(list(range(blocks)), [rows_in])]
        key_blocks = [me]

    results = []
    for number, (query_blocks, pieces) in enumerate(phases):
        head = jnp.stack([jnp.int32(b) for b in key_blocks + query_blocks])
        numbers = jnp.concatenate([head, new_counts.reshape(-1), cache_counts.reshape(-1)])
        for i in range(kv):
            near_queries = paired and number == 0
            results.append(
                attend(
                    numbers, packed[i], pieces, cols, i, sizes, len(query_blocks), near_queries
                )
            )

    halving = heads == 4
    order = jnp.asarray([0, 2, 1, 3] if halving else list(range(heads)), jnp.int32)
    row_blocks = jnp.stack([jnp.int32(b) for p in phases for b in p[0]])
    pick = (row_blocks[:, None] == jnp.arange(blocks, dtype=jnp.int32)[None, :]).astype(jnp.int32)
    dest = jnp.sum(pick[:, :, None] * row_dest.reshape(1, blocks, block_rows), axis=1).reshape(-1)
    out_rows = all_rows // heads
    dest_head = dest // out_rows
    dest_head = dest_head ^ my_head if even else (dest_head - my_head) % heads
    place = jnp.sum((order[None, :] == dest_head[:, None]) * jnp.arange(heads)[None, :], axis=1)
    dest = (place * out_rows + dest % out_rows)[None, :].astype(jnp.int32)

    if paired:
        parts = []
        for i in range(kv):
            own, other = results[i], results[kv + i]
            from_own = [lax.ppermute(a, "ctx", far) for a in own]
            from_other = [lax.ppermute(a, "ctx", far) for a in other]
            parts.append(
                combine(
                    dest,
                    [
                        (own[0], from_other[0], own[1], from_other[1]),
                        (other[0], from_own[0], other[1], from_own[1]),
                    ],
                )
            )
        mine, others = parts, [lax.ppermute(a, "ctx", near) for a in parts]
        mine_rows = jnp.stack([half * kv + i for i in range(kv)])
        other_rows = jnp.stack([(1 - half) * kv + i for i in range(kv)])
    else:
        parts = []
        group = cols // HEAD_DIM
        landing = (jnp.arange(all_rows)[:, None] == dest).astype(jnp.bfloat16)
        for part, stat in results:
            got = lax.all_to_all(part.reshape(blocks, block_rows, cols), "ctx", 0, 0, tiled=True)
            logs = lax.all_to_all(stat.reshape(blocks, block_rows, 128), "ctx", 0, 0, tiled=True)
            logs = logs.reshape(blocks, block_rows, 128)[..., :group]
            share = jnp.exp(logs - jnp.max(logs, axis=0)[None])
            share = share / jnp.sum(share, axis=0)[None]
            stacked = got.reshape(blocks, block_rows, group, HEAD_DIM).astype(jnp.float32)
            mine = jnp.sum(share[..., None] * stacked, axis=0).astype(jnp.bfloat16)
            mine = lax.all_gather(mine.reshape(block_rows, cols), "ctx", axis=0, tiled=True)
            parts.append(jnp.dot(landing, mine, preferred_element_type=jnp.float32).astype(jnp.bfloat16))

    if not paired:
        mine, others = parts, []
        mine_rows = jnp.arange(kv, dtype=jnp.int32)

    hops = [[(i, i ^ d if even else (i + d) % heads) for i in range(heads)] for d in range(heads)]
    width = out_weight.shape[1] // 2
    step = width // 4
    direct_cuts = [
        (d * out_rows, (d + 1) * out_rows, jnp.bfloat16 if d else jnp.float32) for d in range(heads)
    ]
    pair_cuts = [
        (0, out_rows, jnp.float32),
        (out_rows, 2 * out_rows, jnp.float32),
        (2 * out_rows, 4 * out_rows, jnp.bfloat16),
    ]
    chunks = []
    for number in range(2):
        first = number * width
        by_pairs = halving and number == 0
        cuts = pair_cuts if by_pairs else direct_cuts
        if others and number == 0:
            whole = [(0, all_rows, jnp.float32)]
            begun = project(mine_rows, mine, out_weight, whole, first, width, step)
            shares = project(other_rows, others, out_weight, cuts, first, width, step, begun)
        elif others:
            rows = jnp.concatenate([mine_rows, other_rows])
            shares = project(rows, mine + others, out_weight, cuts, first, width, step)
        else:
            shares = project(mine_rows, mine, out_weight, cuts, first, width, step)
        if by_pairs:
            got = lax.ppermute(shares[2], "head", hops[1])
            away = (shares[1] + got[out_rows:].astype(jnp.float32)).astype(jnp.bfloat16)
            chunks.append([shares[0], got, lax.ppermute(away, "head", hops[2])])
        else:
            if halving:
                shares = [shares[i] for i in (0, 2, 1, 3)]
            chunks.append(
                [shares[0]] + [lax.ppermute(shares[d], "head", hops[d]) for d in range(1, heads)]
            )
    return finish(chunks)


def solution(mesh):
    return jax.shard_map(
        per_device,
        mesh=mesh,
        in_specs=(
            P(("groups", "ctx"), "head"),
            P(("groups", "ctx"), "head"),
            P(("groups", "ctx"), "head"),
            P(("groups", "ctx"), "head"),
            P(("groups", "ctx"), "head"),
            P("head", "ctx"),
            P("groups", None),
            P("groups", None),
            P("groups"),
        ),
        out_specs=P(("groups", "head"), "ctx"),
        check_vma=False,
    )
```

profile of v0, /device:TPU:0, one launch (start us, length us, event | category | flops | bytes accessed | tf_op | source)
XLA Modules:
  0.0 80.6 jit_solution(17967148413723709139)
XLA Ops:
  0.0 1.4 %pack.3 = bf16[4672,128]{1,0:T(8,128)(2,1)S(1)} custom-call(s32[1]{0:T(128)} %bitcast.index.order, bf16[2048,256]{1,0:T(8,128)(2,1)} %refs_0_.3, bf16[2048,256]{1,0:T(8,128)(2,1)} %refs_1_.5, bf16[32,256]{1,0:T(8,128)(2,1)} %refs_2_.4, bf16[32,256]{1,0:T(8,128)(2,1)} %refs_3_.3, bf16[32,4096]{1,0:T(8,128)(2,1)} %q_ref.1), custom_call_target="tpu_custom_call" | custom-call | tf_op jit(solution)/shard_map/pack/pallas_call | solution.py:51
  1.4 0.5 collective-permute-start
  1.9 1.7 %split.1 = (bf16[32,2048]{1,0:T(8,128)(2,1)}, bf16[32,2048]{1,0:T(8,128)(2,1)}) custom-call(s32[1]{0:T(128)} %bitcast.6.index.order, bf16[32,4096]{1,0:T(8,128)(2,1)} %q_ref.1), custom_call_target="tpu_custom_call" | custom-call | tf_op jit(solution)/shard_map/split/pallas_call | solution.py:78
  3.6 2.6 %collective-permute-start.1 = (bf16[32,2048]{1,0:T(8,128)(2,1)}, bf16[32,2048]{1,0:T(8,128)(2,1)}, u32[]{:S(2)}, u32[]{:S(2)}) collective-permute-start(bf16[32,2048]{1,0:T(8,128)(2,1)} %get-tuple-element.18.rest_2_), channel_id=1, source_target_pairs={{0,8},{4,12},{8,0},{12,4},{1,9},{5,13},{9,1},{13,5},{2,10},{6,14},... | collective-permute-start | bytes 393224 | tf_op jit(solution)/shard_map/ppermute | solution.py:437
  6.2 0.0 copy-start
  6.2 0.0 copy-start.1
  6.2 0.0 copy-start.2
  6.2 0.2 collective-permute-start.2
  6.4 1.2 %pack.2.rest_0_ = bf16[4160,128]{1,0:T(8,128)(2,1)S(1)} custom-call(s32[1]{0:T(128)} %bitcast.6.index.order, bf16[2048,256]{1,0:T(8,128)(2,1)} %refs_0_.3, bf16[2048,256]{1,0:T(8,128)(2,1)} %refs_1_.5, bf16[32,256]{1,0:T(8,128)(2,1)} %refs_2_.4, bf16[32,256]{1,0:T(8,128)(2,1)} %refs_3_.3), custom_call_target="tpu_custom_call" | custom-call | tf_op jit(solution)/shard_map/pack/pallas_call | solution.py:51
  7.7 0.0 copy-done
  7.7 0.1 reshape.138
  7.8 0.0 copy-done.1
  7.8 0.1 reshape.139
  7.9 0.0 copy-done.2
  7.9 0.1 mul.38
  7.9 0.1 concatenate.9.numbers
  8.0 0.1 concatenate.10.numbers
  8.1 0.1 pad_add_fusion
  8.2 0.1 fusion
  8.3 0.1 multiply_reduce_fusion
  8.4 0.1 reshape.136
  8.5 2.4 %collective-permute-done.1.rest_2_ = bf16[32,2048]{1,0:T(8,128)(2,1)} collective-permute-done((bf16[32,2048]{1,0:T(8,128)(2,1)}, bf16[32,2048]{1,0:T(8,128)(2,1)}, u32[]{:S(2)}, u32[]{:S(2)}) %collective-permute-start.1) | collective-permute-done | bytes 131104 | tf_op jit(solution)/shard_map/ppermute | solution.py:437
  10.9 2.4 %collective-permute-done.2.rest_3_ = bf16[32,2048]{1,0:T(8,128)(2,1)} collective-permute-done((bf16[32,2048]{1,0:T(8,128)(2,1)}, bf16[32,2048]{1,0:T(8,128)(2,1)}, u32[]{:S(2)}, u32[]{:S(2)}) %collective-permute-start.2) | collective-permute-done | bytes 131104 | tf_op jit(solution)/shard_map/ppermute | solution.py:438
  13.3 0.0 collective-permute-done.rest_1_
  13.3 8.2 %attend.3 = (bf16[64,2048]{1,0:T(8,128)(2,1)S(1)}, f32[64,128]{1,0:T(8,128)S(1)}) custom-call(s32[36]{0:T(128)S(1)} %concatenate.10.numbers, bf16[4160,128]{1,0:T(8,128)(2,1)S(1)} %pack.2.rest_0_, bf16[4672,128]{1,0:T(8,128)(2,1)S(1)} %collective-permute-done.rest_1_, bf16[32,2048]{1,0:T(8,128)(2,1)} %collective-permute-done.1.rest_2_, ...), custom_call_target="tpu_custom_call" | custom-call | flops 1937768448 | bytes 16777216 | tf_op jit(solution)/shard_map/attend/pallas_call | solution.py:259
  21.5 0.0 copy-start.3
  21.5 1.6 %collective-permute-start.3 = (bf16[64,2048]{1,0:T(8,128)(2,1)S(1)}, bf16[64,2048]{1,0:T(8,128)(2,1)S(1)}, u32[]{:S(2)}, u32[]{:S(2)}) collective-permute-start(bf16[64,2048]{1,0:T(8,128)(2,1)S(1)} %get-tuple-element.21.refs_4_), channel_id=1, source_target_pairs={{0,8},{4,12},{8,0},{12,4},{1,9},{5,13},{9,1},{13,5},{2,10},{6,14},... | collective-permute-start | bytes 786440 | tf_op jit(solution)/shard_map/ppermute | solution.py:485
  23.2 8.2 %attend.2 = (bf16[64,2048]{1,0:T(8,128)(2,1)S(1)}, f32[64,128]{1,0:T(8,128)S(1)}) custom-call(s32[36]{0:T(128)S(1)} %concatenate.9.numbers, bf16[4160,128]{1,0:T(8,128)(2,1)S(1)} %pack.2.rest_0_, bf16[4672,128]{1,0:T(8,128)(2,1)S(1)} %collective-permute-done.rest_1_, bf16[32,2048]{1,0:T(8,128)(2,1)} %get-tuple-element.18.rest_2_), custom_call_target="tpu_custom_call" | custom-call | flops 1937768448 | bytes 16777216 | tf_op jit(solution)/shard_map/attend/pallas_call | solution.py:259
  31.3 0.5 collective-permute-start.5
  31.9 0.0 copy-done.3
  31.9 0.1 select_reduce_fusion
  32.0 0.1 reshape.137
  32.0 1.5 %collective-permute-start.4 = (f32[64,128]{1,0:T(8,128)S(1)}, f32[64,128]{1,0:T(8,128)S(1)}, u32[]{:S(2)}, u32[]{:S(2)}) collective-permute-start(f32[64,128]{1,0:T(8,128)S(1)} %get-tuple-element.23.refs_6_), channel_id=1, source_target_pairs={{0,8},{4,12},{8,0},{12,4},{1,9},{5,13},{9,1},{13,5},{2,10},{6,14},... | collective-permute-start | bytes 98312 | tf_op jit(solution)/shard_map/ppermute | solution.py:485
  33.6 0.5 collective-permute-start.6
  34.1 6.5 %collective-permute-done.4.refs_3_ = f32[64,128]{1,0:T(8,128)S(1)} collective-permute-done((f32[64,128]{1,0:T(8,128)S(1)}, f32[64,128]{1,0:T(8,128)S(1)}, u32[]{:S(2)}, u32[]{:S(2)}) %collective-permute-start.4) | collective-permute-done | bytes 32800 | tf_op jit(solution)/shard_map/ppermute | solution.py:485
  40.6 0.4 collective-permute-done.6.refs_7_
  40.9 0.0 collective-permute-done.3.refs_1_
  40.9 0.0 collective-permute-done.5.refs_5_
  40.9 0.9 %combine.1.refs_0_ = bf16[128,2048]{1,0:T(8,128)(2,1)S(1)} custom-call(s32[1,128]{1,0:T(1,128)S(1)} %fusion.1.dest_ref, bf16[64,2048]{1,0:T(8,128)(2,1)S(1)} %get-tuple-element.19.refs_0_, bf16[64,2048]{1,0:T(8,128)(2,1)S(1)} %collective-permute-done.3.refs_1_, f32[64,128]{1,0:T(8,128)S(1)} %get-tuple-element.22.refs_2_, ...), custom_call_target="tpu_custom_call" | custom-call | tf_op jit(solution)/shard_map/combine/pallas_call | solution.py:316
  41.8 0.1 collective-permute-start.7
  41.9 4.0 %project.3.refs_2_ = f32[128,2048]{1,0:T(8,128)S(1)} custom-call(s32[1]{0:T(128)} %bitcast.6.index.order, bf16[128,2048]{1,0:T(8,128)(2,1)S(1)} %combine.1.refs_0_, bf16[4096,4096]{1,0:T(8,128)(2,1)} %refs_2_.5), custom_call_target="tpu_custom_call" | custom-call | flops 1073741824 | bytes 8388608 | tf_op jit(solution)/shard_map/project/pallas_call | solution.py:356
  45.9 0.0 collective-permute-done.7.refs_0_.refs_1_
  45.9 4.0 %project.4 = (f32[32,2048]{1,0:T(8,128)S(1)}, f32[32,2048]{1,0:T(8,128)S(1)}, bf16[64,2048]{1,0:T(8,128)(2,1)S(1)}) custom-call(s32[1]{0:T(128)} %bitcast.index.order, bf16[128,2048]{1,0:T(8,128)(2,1)S(1)} %collective-permute-done.7.refs_0_.refs_1_, bf16[4096,4096]{1,0:T(8,128)(2,1)} %refs_2_.5, f32[128,2048]{1,0:T(8,128)S(1)} %project.3.refs_2_), custom_call_target="tpu_custom_call" | custom-call | flops 1073741824 | bytes 8388608 | tf_op jit(solution)/shard_map/project/pallas_call | solution.py:356
  49.9 1.6 %collective-permute-start.8 = (bf16[64,2048]{1,0:T(8,128)(2,1)S(1)}, bf16[64,2048]{1,0:T(8,128)(2,1)S(1)}, u32[]{:S(2)}, u32[]{:S(2)}) collective-permute-start(bf16[64,2048]{1,0:T(8,128)(2,1)S(1)} %get-tuple-element.25), channel_id=1, source_target_pairs={{0,1},{1,0},{2,3},{3,2},{4,5},{5,4},{6,7},{7,6},{8,9},{9,8},{10,11... | collective-permute-start | bytes 786440 | tf_op jit(solution)/shard_map/ppermute | solution.py:543
  51.6 0.1 pad_add_fusion.1.order
  51.6 7.3 %project.5 = (f32[32,2048]{1,0:T(8,128)S(1)}, bf16[32,2048]{1,0:T(8,128)(2,1)S(1)}, bf16[32,2048]{1,0:T(8,128)(2,1)S(1)}, bf16[32,2048]{1,0:T(8,128)(2,1)S(1)}) custom-call(s32[2]{0:T(128)S(1)} %pad_add_fusion.1.order, bf16[128,2048]{1,0:T(8,128)(2,1)S(1)} %combine.1.refs_0_, bf16[128,2048]{1,0:T(8,128)(2,1)S(1)} %collective-permute-done.7.refs_0_.refs_1_, ...), custom_call_target="tpu_custom_call" | custom-call | flops 2147483648 | bytes 16777216 | tf_op jit(solution)/shard_map/project/pallas_call | solution.py:356
  59.0 0.5 collective-permute-start.10
  59.5 2.6 %collective-permute-start.11 = (bf16[32,2048]{1,0:T(8,128)(2,1)S(1)}, bf16[32,2048]{1,0:T(8,128)(2,1)S(1)}, u32[]{:S(2)}, u32[]{:S(2)}) collective-permute-start(bf16[32,2048]{1,0:T(8,128)(2,1)S(1)} %get-tuple-element.29), channel_id=1, source_target_pairs={{0,2},{1,3},{2,0},{3,1},{4,6},{5,7},{6,4},{7,5},{8,10},{9,11},{10,... | collective-permute-start | bytes 393224 | tf_op jit(solution)/shard_map/ppermute | solution.py:550
  62.1 1.3 %collective-permute-start.12 = (bf16[32,2048]{1,0:T(8,128)(2,1)S(1)}, bf16[32,2048]{1,0:T(8,128)(2,1)S(1)}, u32[]{:S(2)}, u32[]{:S(2)}) collective-permute-start(bf16[32,2048]{1,0:T(8,128)(2,1)S(1)} %get-tuple-element.30), channel_id=1, source_target_pairs={{0,3},{1,2},{2,1},{3,0},{4,7},{5,6},{6,5},{7,4},{8,11},{9,10},{10,... | collective-permute-start | bytes 393224 | tf_op jit(solution)/shard_map/ppermute | solution.py:550
  63.4 0.0 collective-permute-done.8.refs_1_
  63.5 1.8 %collective-permute-start.9 = (bf16[32,2048]{1,0:T(8,128)(2,1)S(1)}, bf16[32,2048]{1,0:T(8,128)(2,1)S(1)}, u32[]{:S(2)}, u32[]{:S(2)}) collective-permute-start(bf16[32,2048]{1,0:T(8,128)(2,1)S(1)} %add_convert_fusion), channel_id=1, source_target_pairs={{0,2},{1,3},{2,0},{3,1},{4,6},{5,7},{6,4},{7,5},{8,10},{9,11},{10,... | collective-permute-start | bytes 393224 | tf_op jit(solution)/shard_map/ppermute | solution.py:545
  65.2 2.2 %collective-permute-done.10.refs_4_ = bf16[32,2048]{1,0:T(8,128)(2,1)S(1)} collective-permute-done((bf16[32,2048]{1,0:T(8,128)(2,1)S(1)}, bf16[32,2048]{1,0:T(8,128)(2,1)S(1)}, u32[]{:S(2)}, u32[]{:S(2)}) %collective-permute-start.10) | collective-permute-done | bytes 131104 | tf_op jit(solution)/shard_map/ppermute | solution.py:550
  67.5 0.0 collective-permute-done.11.refs_5_
  67.5 5.7 %collective-permute-done.12.refs_6_ = bf16[32,2048]{1,0:T(8,128)(2,1)S(1)} collective-permute-done((bf16[32,2048]{1,0:T(8,128)(2,1)S(1)}, bf16[32,2048]{1,0:T(8,128)(2,1)S(1)}, u32[]{:S(2)}, u32[]{:S(2)}) %collective-permute-start.12) | collective-permute-done | bytes 131104 | tf_op jit(solution)/shard_map/ppermute | solution.py:550
  73.1 6.7 %collective-permute-done.9.refs_2_ = bf16[32,2048]{1,0:T(8,128)(2,1)S(1)} collective-permute-done((bf16[32,2048]{1,0:T(8,128)(2,1)S(1)}, bf16[32,2048]{1,0:T(8,128)(2,1)S(1)}, u32[]{:S(2)}, u32[]{:S(2)}) %collective-permute-start.9) | collective-permute-done | bytes 131104 | tf_op jit(solution)/shard_map/ppermute | solution.py:545
  79.8 0.8 finish.1
  (3 shorter events, 0.0 us)
Async XLA Ops:
  1.4 11.9 %collective-permute-start = (bf16[4672,128]{1,0:T(8,128)(2,1)S(1)}, bf16[4672,128]{1,0:T(8,128)(2,1)S(1)}, u32[]{:S(2)}, u32[]{:S(2)}) collective-permute-start(bf16[4672,128]{1,0:T(8,128)(2,1)S(1)} %pack.3), channel_id=1, source_target_pairs={{0,4},{4,0},{8,12},{12,8},{1,5},{5,1},{9,13},{13,9},{2,6},{6,2},{1... | collective-permute-start | bytes 3588104 | tf_op jit(solution)/shard_map/ppermute | solution.py:442
  3.6 7.3 %collective-permute-start.1 = (bf16[32,2048]{1,0:T(8,128)(2,1)}, bf16[32,2048]{1,0:T(8,128)(2,1)}, u32[]{:S(2)}, u32[]{:S(2)}) collective-permute-start(bf16[32,2048]{1,0:T(8,128)(2,1)} %get-tuple-element.18.rest_2_), channel_id=1, source_target_pairs={{0,8},{4,12},{8,0},{12,4},{1,9},{5,13},{9,1},{13,5},{2,10},{6,14},... | collective-permute-start | bytes 393224 | tf_op jit(solution)/shard_map/ppermute | solution.py:437
  6.2 1.5 %copy-start = (s32[4,4]{1,0:T(4,128)S(1)}, s32[4,4]{1,0:T(4,128)}, u32[]{:S(2)}) copy-start(s32[4,4]{1,0:T(4,128)} %param.16) | copy-start | bytes 196
  6.2 1.6 %copy-start.1 = (s32[4,4]{1,0:T(4,128)S(1)}, s32[4,4]{1,0:T(4,128)}, u32[]{:S(2)}) copy-start(s32[4,4]{1,0:T(4,128)} %param.17) | copy-start | bytes 196
  6.2 1.6 %copy-start.2 = (s32[128]{0:T(128)S(1)}, s32[128]{0:T(128)}, u32[]{:S(2)}) copy-start(s32[128]{0:T(128)} %param.18) | copy-start | bytes 1540
  6.2 7.1 %collective-permute-start.2 = (bf16[32,2048]{1,0:T(8,128)(2,1)}, bf16[32,2048]{1,0:T(8,128)(2,1)}, u32[]{:S(2)}, u32[]{:S(2)}) collective-permute-start(bf16[32,2048]{1,0:T(8,128)(2,1)} %get-tuple-element.20), channel_id=1, source_target_pairs={{0,12},{4,8},{8,4},{12,0},{1,13},{5,9},{9,5},{13,1},{2,14},{6,10},... | collective-permute-start | bytes 393224 | tf_op jit(solution)/shard_map/ppermute | solution.py:438
  21.5 10.4 %copy-start.3 = (s32[4]{0:T(128)S(1)}, s32[4]{0:T(128)}, u32[]{:S(2)}) copy-start(s32[4]{0:T(128)} %constant.54.clone) | copy-start | bytes 52
  21.5 19.4 %collective-permute-start.3 = (bf16[64,2048]{1,0:T(8,128)(2,1)S(1)}, bf16[64,2048]{1,0:T(8,128)(2,1)S(1)}, u32[]{:S(2)}, u32[]{:S(2)}) collective-permute-start(bf16[64,2048]{1,0:T(8,128)(2,1)S(1)} %get-tuple-element.21.refs_4_), channel_id=1, source_target_pairs={{0,8},{4,12},{8,0},{12,4},{1,9},{5,13},{9,1},{13,5},{2,10},{6,14},... | collective-permute-start | bytes 786440 | tf_op jit(solution)/shard_map/ppermute | solution.py:485
  31.3 9.6 %collective-permute-start.5 = (bf16[64,2048]{1,0:T(8,128)(2,1)S(1)}, bf16[64,2048]{1,0:T(8,128)(2,1)S(1)}, u32[]{:S(2)}, u32[]{:S(2)}) collective-permute-start(bf16[64,2048]{1,0:T(8,128)(2,1)S(1)} %get-tuple-element.19.refs_0_), channel_id=1, source_target_pairs={{0,8},{4,12},{8,0},{12,4},{1,9},{5,13},{9,1},{13,5},{2,10},{6,14},... | collective-permute-start | bytes 786440 | tf_op jit(solution)/shard_map/ppermute | solution.py:484
  32.0 8.5 %collective-permute-start.4 = (f32[64,128]{1,0:T(8,128)S(1)}, f32[64,128]{1,0:T(8,128)S(1)}, u32[]{:S(2)}, u32[]{:S(2)}) collective-permute-start(f32[64,128]{1,0:T(8,128)S(1)} %get-tuple-element.23.refs_6_), channel_id=1, source_target_pairs={{0,8},{4,12},{8,0},{12,4},{1,9},{5,13},{9,1},{13,5},{2,10},{6,14},... | collective-permute-start | bytes 98312 | tf_op jit(solution)/shard_map/ppermute | solution.py:485
  33.6 7.3 %collective-permute-start.6 = (f32[64,128]{1,0:T(8,128)S(1)}, f32[64,128]{1,0:T(8,128)S(1)}, u32[]{:S(2)}, u32[]{:S(2)}) collective-permute-start(f32[64,128]{1,0:T(8,128)S(1)} %get-tuple-element.22.refs_2_), channel_id=1, source_target_pairs={{0,8},{4,12},{8,0},{12,4},{1,9},{5,13},{9,1},{13,5},{2,10},{6,14},... | collective-permute-start | bytes 98312 | tf_op jit(solution)/shard_map/ppermute | solution.py:484
  41.8 4.1 %collective-permute-start.7 = (bf16[128,2048]{1,0:T(8,128)(2,1)S(1)}, bf16[128,2048]{1,0:T(8,128)(2,1)S(1)}, u32[]{:S(2)}, u32[]{:S(2)}) collective-permute-start(bf16[128,2048]{1,0:T(8,128)(2,1)S(1)} %combine.1.refs_0_), channel_id=1, source_target_pairs={{0,4},{4,0},{8,12},{12,8},{1,5},{5,1},{9,13},{13,9},{2,6},{6,2},{1... | collective-permute-start | bytes 1572872 | tf_op jit(solution)/shard_map/ppermute | solution.py:495
  49.9 13.5 %collective-permute-start.8 = (bf16[64,2048]{1,0:T(8,128)(2,1)S(1)}, bf16[64,2048]{1,0:T(8,128)(2,1)S(1)}, u32[]{:S(2)}, u32[]{:S(2)}) collective-permute-start(bf16[64,2048]{1,0:T(8,128)(2,1)S(1)} %get-tuple-element.25), channel_id=1, source_target_pairs={{0,1},{1,0},{2,3},{3,2},{4,5},{5,4},{6,7},{7,6},{8,9},{9,8},{10,11... | collective-permute-start | bytes 786440 | tf_op jit(solution)/shard_map/ppermute | solution.py:543
  59.0 8.5 %collective-permute-start.10 = (bf16[32,2048]{1,0:T(8,128)(2,1)S(1)}, bf16[32,2048]{1,0:T(8,128)(2,1)S(1)}, u32[]{:S(2)}, u32[]{:S(2)}) collective-permute-start(bf16[32,2048]{1,0:T(8,128)(2,1)S(1)} %get-tuple-element.28), channel_id=1, source_target_pairs={{0,1},{1,0},{2,3},{3,2},{4,5},{5,4},{6,7},{7,6},{8,9},{9,8},{10,11... | collective-permute-start | bytes 393224 | tf_op jit(solution)/shard_map/ppermute | solution.py:550
  59.5 8.0 %collective-permute-start.11 = (bf16[32,2048]{1,0:T(8,128)(2,1)S(1)}, bf16[32,2048]{1,0:T(8,128)(2,1)S(1)}, u32[]{:S(2)}, u32[]{:S(2)}) collective-permute-start(bf16[32,2048]{1,0:T(8,128)(2,1)S(1)} %get-tuple-element.29), channel_id=1, source_target_pairs={{0,2},{1,3},{2,0},{3,1},{4,6},{5,7},{6,4},{7,5},{8,10},{9,11},{10,... | collective-permute-start | bytes 393224 | tf_op jit(solution)/shard_map/ppermute | solution.py:550
  62.1 11.0 %collective-permute-start.12 = (bf16[32,2048]{1,0:T(8,128)(2,1)S(1)}, bf16[32,2048]{1,0:T(8,128)(2,1)S(1)}, u32[]{:S(2)}, u32[]{:S(2)}) collective-permute-start(bf16[32,2048]{1,0:T(8,128)(2,1)S(1)} %get-tuple-element.30), channel_id=1, source_target_pairs={{0,3},{1,2},{2,1},{3,0},{4,7},{5,6},{6,5},{7,4},{8,11},{9,10},{10,... | collective-permute-start | bytes 393224 | tf_op jit(solution)/shard_map/ppermute | solution.py:550
  63.5 16.4 %collective-permute-start.9 = (bf16[32,2048]{1,0:T(8,128)(2,1)S(1)}, bf16[32,2048]{1,0:T(8,128)(2,1)S(1)}, u32[]{:S(2)}, u32[]{:S(2)}) collective-permute-start(bf16[32,2048]{1,0:T(8,128)(2,1)S(1)} %add_convert_fusion), channel_id=1, source_target_pairs={{0,2},{1,3},{2,0},{3,1},{4,6},{5,7},{6,4},{7,5},{8,10},{9,11},{10,... | collective-permute-start | bytes 393224 | tf_op jit(solution)/shard_map/ppermute | solution.py:545
where the time goes:
time: 80.8 us; the launch traced here: 80.6 us
  Pallas kernels  37.7 us (47%)
  waiting for transfers between devices  26.3 us (33%)
  starting transfers between devices  15.4 us (19%)
    pallas_call x2, Pallas kernels, attend(): pl.pallas_call(functools.partial(attention_kernel, blocks, sets, query_bl...  16.4 us
    pallas_call x3, Pallas kernels, project(): pl.pallas_call(functools.partial(project_kernel, len(parts), len(added),...  15.3 us
    ppermute x3, waiting for transfers between devices, per_device(): lax.ppermute(shares[d], 'head', hops[d])  7.9 us
    ppermute x1, waiting for transfers between devices, per_device(): chunks.append([shares[0], got, lax.ppermute(away, 'head', hops[2])])  6.69 us
    ppermute x2, waiting for transfers between devices, per_device(): from_other = [lax.ppermute(a, 'ctx', far) for a in other]  6.5 us
    ppermute x3, starting transfers between devices, per_device(): lax.ppermute(shares[d], 'head', hops[d])  4.45 us
    ppermute x2, starting transfers between devices, per_device(): from_other = [lax.ppermute(a, 'ctx', far) for a in other]  3.16 us
    pallas_call x2, Pallas kernels, pack(): pl.pallas_call(functools.partial(pack_kernel, number, kv), in_specs=[pl.B...  2.64 us
  transfers between devices with their start and end apart: 13, of which 7 were waited for; matrix products, arithmetic and copies ran while one was open for 1% of the time, Pallas kernels for 28%

commit v1 on v0

v1 whole, which is shorter than its diff:
```python
import functools
import math

import jax
import jax.numpy as jnp
from jax import lax
from jax.experimental import pallas as pl
from jax.experimental.pallas import tpu as pltpu
from jax.sharding import PartitionSpec as P

HEAD_DIM = 128
CAPR = 512
ROWS = 16
ALIGN = 16
NEG = -1e30
SCALE = 1.0 / math.sqrt(HEAD_DIM)
LOG2E = math.log2(math.e)
SPANS = 2
COPIES = 4


def in_hbm(a):
    return pltpu.with_memory_space_constraint(a, pltpu.HBM)


def my_half():
    return lax.rem(lax.axis_index("ctx"), 2)


def pack_kernel(number, kv, other, *refs):
    sources, out_ref, sems = refs[:-2], refs[-2], refs[-1]
    block = (1 - my_half() if other else my_half()) * kv + number
    copies = []
    at = 0
    for ref in sources[:4]:
        rows = ref.shape[0]
        columns = pl.ds(pl.multiple_of(block * HEAD_DIM, HEAD_DIM), HEAD_DIM)
        copies.append((ref.at[:, columns], out_ref.at[at : at + rows, :]))
        at += rows
    for ref in sources[4:]:
        rows = ref.shape[0]
        heads = (out_ref.shape[0] - at) // rows
        for g in range(heads):
            columns = pl.ds(pl.multiple_of((block * heads + g) * HEAD_DIM, HEAD_DIM), HEAD_DIM)
            copies.append((ref.at[:, columns], out_ref.at[at : at + rows, :]))
            at += rows
    copies = [pltpu.make_async_copy(a, b, sems.at[n]) for n, (a, b) in enumerate(copies)]
    for c in copies:
        c.start()
    for c in copies:
        c.wait()


def pack(other, arrays, queries, kv, number):
    group = queries[0].shape[1] // arrays[0].shape[1] if queries else 0
    rows = sum(a.shape[0] for a in arrays) + sum(q.shape[0] * group for q in queries)
    return pl.pallas_call(
        functools.partial(pack_kernel, number, kv, other),
        in_specs=[pl.BlockSpec(memory_space=pltpu.HBM)] * (len(arrays) + len(queries)),
        out_specs=pl.BlockSpec(memory_space=pltpu.VMEM),
        out_shape=jax.ShapeDtypeStruct((rows, HEAD_DIM), arrays[0].dtype),
        scratch_shapes=[pltpu.SemaphoreType.DMA((len(arrays) + group,))],
        compiler_params=pltpu.CompilerParams(vmem_limit_bytes=4 * 2**20),
        name="pack",
    )(*[in_hbm(a) for a in (*arrays, *queries)])


def split_kernel(q_ref, *refs):
    outs, sems = refs[:-1], refs[-1]
    width = outs[0].shape[1]
    copies = []
    for n, out in enumerate(outs):
        columns = pl.ds(pl.multiple_of((my_half() ^ n) * width, width), width)
        copies.append(pltpu.make_async_copy(q_ref.at[:, columns], out, sems.at[n]))
    for c in copies:
        c.start()
    for c in copies:
        c.wait()


def split(a):
    half = jax.ShapeDtypeStruct((a.shape[0], a.shape[1] // 2), a.dtype)
    return pl.pallas_call(
        split_kernel,
        in_specs=[pl.BlockSpec(memory_space=pltpu.HBM)],
        out_specs=[pl.BlockSpec(memory_space=pltpu.VMEM)] * 2,
        out_shape=[half, half],
        scratch_shapes=[pltpu.SemaphoreType.DMA((2,))],
        compiler_params=pltpu.CompilerParams(vmem_limit_bytes=2 * 2**20),
        name="split",
    )(in_hbm(a))


def attention_kernel(
    key_blocks, query_blocks, number, window, shard_rows, block_rows, near_queries, weight_block,
    new_ref, cache_ref, weight_ref, *rest,
):
    key_blocks, row_blocks = key_blocks(), query_blocks()
    shards = len(key_blocks)
    query_blocks = len(row_blocks)
    reqs = new_ref.shape[1]
    packed = rest[:shards]
    q_refs = rest[shards : -4 - SPANS]
    out_ref, held = rest[-4 - SPANS], rest[-3 - SPANS : -3]
    sorted_q, part, sems = rest[-3:]
    copies = []
    for j, there in enumerate(held):
        rows, width = there.shape
        share = rows // COPIES
        for n in range(COPIES):
            first = pl.multiple_of(weight_block() * rows + n * share, ALIGN)
            source = weight_ref.at[pl.ds(first, share), j * width : (j + 1) * width]
            target = there.at[n * share : (n + 1) * share, :]
            copies.append(pltpu.make_async_copy(source, target, sems.at[len(copies)]))
            copies[-1].start()
    padded = sorted_q.shape[0]
    cols = sorted_q.shape[1]
    group = cols // HEAD_DIM
    all_rows = out_ref.shape[0]

    def new_counts(b, r):
        return new_ref[b, r]

    def cache_counts(b, r):
        return cache_ref[b, r]

    starts = [[jnp.int32(0)] for _ in row_blocks]
    bases = [[] for _ in row_blocks]
    tile_ends = []
    last = jnp.int32(0)
    for r in range(reqs):
        amount = jnp.int32(0)
        for b, block in enumerate(row_blocks):
            bases[b].append(amount)
            amount = amount + new_counts(block, r)
            starts[b].append(starts[b][-1] + new_counts(block, r))
        last = last + (amount + (ROWS - 1)) // ROWS
        tile_ends.append(last)
    tile_starts = [jnp.int32(0)] + tile_ends[:-1]

    offset = lax.broadcasted_iota(jnp.int32, (1, all_rows), 1)
    pos = jnp.zeros((1, all_rows), jnp.int32)
    for b in range(query_blocks):
        here = offset - b * block_rows
        for r in range(reqs):
            mine = (here >= starts[b][r]) & (here < starts[b][r + 1])
            mine = mine & (here >= 0) & (here < block_rows)
            first = tile_starts[r] * ROWS + bases[b][r] - starts[b][r]
            pos = jnp.where(mine, first + here, pos)
    sorter = (lax.broadcasted_iota(jnp.int32, (padded, all_rows), 0) == pos).astype(jnp.bfloat16)
    rows_in = [q[:, number * cols : (number + 1) * cols] for q in q_refs]
    if near_queries:
        first = 2 * (shard_rows + block_rows)
        near = [
            packed[1][first + g * block_rows : first + (g + 1) * block_rows, :]
            for g in range(group)
        ]
        rows_in.insert(1, jnp.concatenate(near, axis=1))
    rows_in = jnp.concatenate(rows_in, axis=0)
    sorted_q[...] = jnp.dot(sorter, rows_in, preferred_element_type=jnp.float32).astype(
        jnp.bfloat16
    )
    part[...] = jnp.zeros_like(part)

    width = shards * (window + block_rows)
    plain = (shards * window) // 128 * 128
    key = lax.broadcasted_iota(jnp.int32, (1, width), 1)
    lane = lax.broadcasted_iota(jnp.int32, (ROWS, 128), 1)
    ones = jnp.ones((width, HEAD_DIM), jnp.bfloat16)

    def tile(i, carry):
        r = jnp.int32(0)
        start_tile = jnp.int32(0)
        for e in tile_ends[:-1]:
            r = r + (i >= e).astype(jnp.int32)
            start_tile = jnp.where(i >= e, e, start_tile)
        inside = None
        key_pos = jnp.full((1, width), -1, jnp.int32)
        ks, vs = [], []
        for j in range(shards):
            shard = key_blocks[j]
            low = jnp.int32(0)
            new_low = jnp.int32(0)
            for o in range(reqs - 1):
                low = low + jnp.where(o < r, cache_counts(shard, o), 0)
                new_low = new_low + jnp.where(o < r, new_counts(shard, o), 0)
            high = low + cache_counts(shard, r)
            new_high = new_low + new_counts(shard, r)
            start = jnp.clip(low // ALIGN * ALIGN, 0, shard_rows - window)
            start = pl.multiple_of(start, ALIGN)
            ks.append(packed[j][pl.ds(start, window), :])
            vs.append(packed[j][pl.ds(pl.multiple_of(start + shard_rows, ALIGN), window), :])
            first = key - j * window + start
            seen = (key >= j * window) & (key < (j + 1) * window)
            seen = seen & (first >= low) & (first < high)
            inside = seen if inside is None else inside | seen
            base = shards * window + j * block_rows
            fresh = key - base
            seen = (key >= base) & (fresh < block_rows)
            key_pos = jnp.where(seen, shard * block_rows + fresh, key_pos)
            inside = inside | (seen & (fresh >= new_low) & (fresh < new_high))
        after = 2 * shard_rows
        for j in range(shards):
            ks.append(packed[j][after : after + block_rows, :])
            vs.append(packed[j][after + block_rows : after + 2 * block_rows, :])
        ks = jnp.concatenate(ks, axis=0)
        vs = jnp.concatenate(vs, axis=0)
        row0 = pl.multiple_of(i * ROWS, ROWS)
        q = jnp.concatenate(
            [
                sorted_q[pl.ds(row0, ROWS), g * HEAD_DIM : (g + 1) * HEAD_DIM]
                for g in range(group)
            ],
            axis=0,
        )
        scores = lax.dot_general(
            q, ks, (((1,), (1,)), ((), ())), preferred_element_type=jnp.float32
        )
        bias = jnp.where(inside, 0.0, NEG)
        t = jnp.zeros((ROWS, 1), jnp.int32)
        among = (i - start_tile) * ROWS + lax.broadcasted_iota(jnp.int32, (ROWS, 1), 0)
        base = jnp.int32(0)
        for block in row_blocks:
            begin = jnp.int32(0)
            for o in range(reqs - 1):
                begin = begin + jnp.where(o < r, new_counts(block, o), 0)
            t = jnp.where(among >= base, block * block_rows + begin + among - base, t)
            base = base + new_counts(block, r)
        causal = jnp.where(key_pos[:, plain:] <= t, bias[:, plain:], NEG)
        causal = jnp.concatenate([causal] * group, axis=0)
        scores = jnp.concatenate(
            [scores[:, :plain] + bias[:, :plain], scores[:, plain:] + causal], axis=1
        )
        top = jnp.max(scores, axis=1, keepdims=True)
        probs = jnp.exp2((scores - top) * (SCALE * LOG2E)).astype(jnp.bfloat16)
        mixed = jnp.dot(
            probs,
            jnp.concatenate([vs, ones], axis=1),
            preferred_element_type=jnp.float32,
        )
        total = mixed[:, HEAD_DIM:]
        value = (mixed[:, :HEAD_DIM] / total).astype(jnp.bfloat16)
        lse = top * SCALE + jnp.log(total)
        logs = jnp.zeros((ROWS, 128), jnp.float32)
        for g in range(group):
            rows = slice(g * ROWS, (g + 1) * ROWS)
            part[pl.ds(row0, ROWS), g * HEAD_DIM : (g + 1) * HEAD_DIM] = value[rows]
            logs = jnp.where(lax.rem(lane, group) == g, lse[rows], logs)
        high = logs.astype(jnp.bfloat16)
        rest_of = logs - high.astype(jnp.float32)
        middle = rest_of.astype(jnp.bfloat16)
        low = rest_of - middle.astype(jnp.float32)
        logs = jnp.where(lane < 2 * group, middle.astype(jnp.float32), low)
        logs = jnp.where(lane < group, high.astype(jnp.float32), logs)
        part[pl.ds(row0, ROWS), cols:] = logs.astype(jnp.bfloat16)
        return carry

    lax.fori_loop(0, last, tile, jnp.int32(0))

    back = (((0,), (0,)), ((), ()))
    out_ref[...] = lax.dot_general(
        sorter, part[...], back, preferred_element_type=jnp.float32
    ).astype(jnp.bfloat16)
    for c in copies:
        c.wait()


def attend(
    counts, packed, queries, cols, number, block_rows, shard_rows, key_blocks, query_blocks, near_queries,
    weight, weight_block,
):
    all_rows = len(query_blocks()) * block_rows
    reqs = counts[0].shape[1]
    padded = (all_rows + reqs * (ROWS - 1)) // ROWS * ROWS
    sets = len(packed)
    window = min(CAPR + ALIGN, shard_rows)
    vmem = pl.BlockSpec(memory_space=pltpu.VMEM)
    return pl.pallas_call(
        functools.partial(
            attention_kernel,
            key_blocks, query_blocks, number, window, shard_rows, block_rows, near_queries, weight_block,
        ),
        in_specs=[pl.BlockSpec(memory_space=pltpu.SMEM)] * 2
        + [pl.BlockSpec(memory_space=pltpu.HBM)]
        + [vmem] * (sets + len(queries)),
        out_specs=[vmem] * (1 + SPANS),
        scratch_shapes=[
            pltpu.VMEM((padded, cols), jnp.bfloat16),
            pltpu.VMEM((padded, cols + 128), jnp.bfloat16),
            pltpu.SemaphoreType.DMA((SPANS * COPIES,)),
        ],
        out_shape=[
            jax.ShapeDtypeStruct((all_rows, cols + 128), jnp.bfloat16),
            *[pltpu.VMEM((cols, weight.shape[1] // SPANS), weight.dtype)] * SPANS,
        ],
        compiler_params=pltpu.CompilerParams(vmem_limit_bytes=8 * 2**20),
        cost_estimate=pl.CostEstimate(
            flops=8 * padded * cols * sets * window,
            bytes_accessed=16 * 2**20,
            transcendentals=0,
        ),
        name="attend",
    )(*[in_hbm(c) for c in counts], in_hbm(weight), *packed, *queries)


def log_sums(pieces, group):
    pieces = pieces.astype(jnp.float32)
    return pieces[..., :group] + pieces[..., group : 2 * group] + pieces[..., 2 * group : 3 * group]


def places(dest, out_rows, heads):
    mine = lax.axis_index("head")
    head = lax.div(dest, out_rows)
    if heads & (heads - 1) == 0:
        head = head ^ mine
    else:
        head = lax.rem(head + heads - mine, heads)
    if heads == 4:
        head = jnp.where(head == 1, 2, jnp.where(head == 2, 1, head))
    return head * out_rows + lax.rem(dest, out_rows)


def combine_kernel(group, heads, dest_ref, *refs):
    sources, out_ref, gathered = refs[:-2], refs[-2], refs[-1]
    rows = out_ref.shape[0]
    cols = group * HEAD_DIM
    me = lax.axis_index("ctx")
    blocks = len(sources)
    block_rows = rows // blocks
    for n in range(0, blocks, 2):
        a_ref, b_ref = sources[n], sources[n + 1]
        sa, sb = log_sums(a_ref[:, cols:], group), log_sums(b_ref[:, cols:], group)
        best = jnp.maximum(sa, sb)
        wa, wb = jnp.exp(sa - best), jnp.exp(sb - best)
        whole = wa + wb
        wa, wb = wa / whole, wb / whole
        for g in range(group):
            at = slice(g * HEAD_DIM, (g + 1) * HEAD_DIM)
            one = wa[:, g : g + 1] * a_ref[:, at].astype(jnp.float32)
            one = one + wb[:, g : g + 1] * b_ref[:, at].astype(jnp.float32)
            one = one.astype(jnp.bfloat16)
            for k in range(2):
                first = pl.multiple_of((me ^ (n + k)) * block_rows, ALIGN)
                gathered[pl.ds(first, block_rows), at] = one[k * block_rows : (k + 1) * block_rows]
    dest = places(dest_ref[...].reshape(1, rows), rows // heads, heads)
    landing = (lax.broadcasted_iota(jnp.int32, (rows, rows), 0) == dest).astype(jnp.bfloat16)
    out_ref[...] = jnp.dot(landing, gathered[...], preferred_element_type=jnp.float32).astype(
        jnp.bfloat16
    )


def combine(dest, arrays, heads):
    vmem = pl.BlockSpec(memory_space=pltpu.VMEM)
    cols = arrays[0].shape[1] - 128
    return pl.pallas_call(
        functools.partial(combine_kernel, cols // HEAD_DIM, heads),
        in_specs=[vmem] * (1 + len(arrays)),
        out_specs=vmem,
        out_shape=jax.ShapeDtypeStruct((dest.shape[0], cols), jnp.bfloat16),
        scratch_shapes=[pltpu.VMEM((dest.shape[0], cols), jnp.bfloat16)],
        compiler_params=pltpu.CompilerParams(vmem_limit_bytes=6 * 2**20),
        name="combine",
    )(dest, *arrays)


def project_kernel(parts, added, cuts, step, *refs):
    a_refs, w_refs = refs[:parts], refs[parts : 2 * parts]
    total_refs, outs = refs[2 * parts : 2 * parts + added], refs[2 * parts + added :]

    def columns(j, carry):
        here = pl.ds(pl.multiple_of(j * step, step), step)
        total = total_refs[0][:, here] if added else None
        for a, w in zip(a_refs, w_refs):
            product = jnp.dot(a[...], w[:, here], preferred_element_type=jnp.float32)
            total = product if total is None else total + product
        for (low, high), out in zip(cuts, outs):
            out[:, here] = total[low:high].astype(out.dtype)
        return carry

    lax.fori_loop(0, outs[0].shape[1] // step, columns, 0)


def project(parts, weights, cuts, step, added=()):
    vmem = pl.BlockSpec(memory_space=pltpu.VMEM)
    depth = parts[0].shape[1] * len(parts)
    width = weights[0].shape[1]
    return pl.pallas_call(
        functools.partial(project_kernel, len(parts), len(added), [c[:2] for c in cuts], step),
        in_specs=[vmem] * (2 * len(parts) + len(added)),
        out_specs=[vmem] * len(cuts),
        out_shape=[jax.ShapeDtypeStruct((high - low, width), dtype) for low, high, dtype in cuts],
        compiler_params=pltpu.CompilerParams(vmem_limit_bytes=6 * 2**20),
        cost_estimate=pl.CostEstimate(
            flops=4 * parts[0].shape[0] * depth * width,
            bytes_accessed=depth * width,
            transcendentals=0,
        ),
        name="project",
    )(*parts, *[pltpu.with_memory_space_constraint(w, pltpu.VMEM) for w in weights], *added)


def finish_kernel(counts, *refs):
    out_ref = refs[-1]
    at = n = 0
    for count in counts:
        rows, width = refs[n].shape
        total = refs[n][...]
        for ref in refs[n + 1 : n + count]:
            total = total + ref[:rows, :].astype(jnp.float32)
        out_ref[:, at : at + width] = total.astype(out_ref.dtype)
        at += width
        n += count


def finish(chunks):
    vmem = pl.BlockSpec(memory_space=pltpu.VMEM)
    arrays = [a for chunk in chunks for a in chunk]
    width = sum(chunk[0].shape[1] for chunk in chunks)
    return pl.pallas_call(
        functools.partial(finish_kernel, [len(chunk) for chunk in chunks]),
        in_specs=[vmem] * len(arrays),
        out_specs=vmem,
        out_shape=jax.ShapeDtypeStruct((arrays[0].shape[0], width), jnp.bfloat16),
        compiler_params=pltpu.CompilerParams(vmem_limit_bytes=8 * 2**20),
        name="finish",
    )(*arrays)


def per_device(
    queries,
    cache_keys,
    cache_values,
    new_keys,
    new_values,
    out_weight,
    new_counts,
    cache_counts,
    row_dest,
):
    blocks = lax.axis_size("ctx")
    heads = lax.axis_size("head")
    block_rows = queries.shape[0]
    all_rows = block_rows * blocks
    kv_here = cache_keys.shape[1] // HEAD_DIM
    paired = blocks == 4 and kv_here % 2 == 0
    even = heads & (heads - 1) == 0
    kv = kv_here // 2 if paired else kv_here
    cols = queries.shape[1] // kv_here
    shard_rows = cache_keys.shape[0]
    caches = (cache_keys, cache_values, new_keys, new_values)

    if paired:
        near = [(i, i ^ 1) for i in range(blocks)]
        far = [(i, i ^ 2) for i in range(blocks)]
        across = [(i, i ^ 3) for i in range(blocks)]
        q_mine, q_other = split(queries)
        q_far = lax.ppermute(q_mine, "ctx", far)
        q_across = lax.ppermute(q_other, "ctx", across)
        packed = [
            [
                pack(False, caches, [], kv, i),
                lax.ppermute(pack(True, caches, [queries], kv, i), "ctx", near),
            ]
            for i in range(kv)
        ]
        nearby = lambda ds: lambda: [lax.axis_index("ctx") ^ d for d in ds]
        phases = [
            (nearby((0, 1)), [q_mine], lambda i: lambda: my_half() * kv + i),
            (nearby((2, 3)), [q_far, q_across], lambda i: lambda: (1 - my_half()) * kv + i),
        ]
        key_blocks = nearby((0, 1))
    else:
        rows_in = lax.all_gather(queries, "ctx", axis=0, tiled=True)
        packed = [
            [jnp.concatenate([a[:, i * HEAD_DIM : (i + 1) * HEAD_DIM] for a in caches], axis=0)]
            for i in range(kv)
        ]
        phases = [(lambda: list(range(blocks)), [rows_in], lambda i: lambda: i)]
        key_blocks = lambda: [lax.axis_index("ctx")]

    counts = (new_counts, cache_counts)
    results = [
        attend(
            counts, packed[i], pieces, cols, i, block_rows, shard_rows, key_blocks, query_blocks,
            paired and number == 0, out_weight, weight_block(i),
        )
        for number, (query_blocks, pieces, weight_block) in enumerate(phases)
        for i in range(kv)
    ]
    weights = [r[1:] for r in results]
    results = [r[0] for r in results]
    halving = heads == 4
    out_rows = all_rows // heads

    if paired:
        mine = []
        for i in range(kv):
            own, other = results[i], results[kv + i]
            from_own, from_other = lax.ppermute(own, "ctx", far), lax.ppermute(other, "ctx", far)
            mine.append(combine(row_dest, [own, from_other, other, from_own], heads))
        others = [lax.ppermute(a, "ctx", near) for a in mine]
    else:
        mine, others = [], []
        group = cols // HEAD_DIM
        landing = jnp.arange(all_rows)[:, None] == places(row_dest, out_rows, heads)[None, :]
        for part in results:
            got = lax.all_to_all(
                part.reshape(blocks, block_rows, cols + 128), "ctx", 0, 0, tiled=True
            ).reshape(blocks, block_rows, cols + 128)
            logs = log_sums(got[..., cols:], group)
            share = jnp.exp(logs - jnp.max(logs, axis=0)[None])
            share = share / jnp.sum(share, axis=0)[None]
            stacked = got[..., :cols].reshape(blocks, block_rows, group, HEAD_DIM)
            one = jnp.sum(share[..., None] * stacked.astype(jnp.float32), axis=0)
            one = one.astype(jnp.bfloat16).reshape(block_rows, cols)
            one = lax.all_gather(one, "ctx", axis=0, tiled=True)
            mine.append(
                jnp.dot(landing.astype(one.dtype), one, preferred_element_type=jnp.float32).astype(
                    one.dtype
                )
            )

    hops = [[(i, i ^ d if even else (i + d) % heads) for i in range(heads)] for d in range(heads)]
    step = out_weight.shape[1] // SPANS // 4
    direct_cuts = [
        (d * out_rows, (d + 1) * out_rows, jnp.bfloat16 if d else jnp.float32) for d in range(heads)
    ]
    pair_cuts = [
        (0, out_rows, jnp.float32),
        (out_rows, 2 * out_rows, jnp.float32),
        (2 * out_rows, 4 * out_rows, jnp.bfloat16),
    ]
    chunks = []
    for number in range(SPANS):
        span = [w[number] for w in weights]
        by_pairs = halving and number == 0
        cuts = pair_cuts if by_pairs else direct_cuts
        if others and number == 0:
            whole = [(0, all_rows, jnp.float32)]
            begun = project(mine, span[:kv], whole, step)
            shares = project(others, span[kv:], cuts, step, begun)
        elif others:
            shares = project(mine + others, span, cuts, step)
        else:
            shares = project(mine, span, cuts, step)
        if by_pairs:
            got = lax.ppermute(shares[2], "head", hops[1])
            away = (shares[1] + got[out_rows:].astype(jnp.float32)).astype(jnp.bfloat16)
            chunks.append([shares[0], got, lax.ppermute(away, "head", hops[2])])
        else:
            if halving:
                shares = [shares[i] for i in (0, 2, 1, 3)]
            chunks.append(
                [shares[0]] + [lax.ppermute(shares[d], "head", hops[d]) for d in range(1, heads)]
            )
    return finish(chunks)


def solution(mesh):
    return jax.shard_map(
        per_device,
        mesh=mesh,
        in_specs=(
            P(("groups", "ctx"), "head"),
            P(("groups", "ctx"), "head"),
            P(("groups", "ctx"), "head"),
            P(("groups", "ctx"), "head"),
            P(("groups", "ctx"), "head"),
            P("head", "ctx"),
            P("groups", None),
            P("groups", None),
            P("groups"),
        ),
        out_specs=P(("groups", "head"), "ctx"),
        check_vma=False,
    )
```

time: 80.8 us -> 68.4 us (0.85)
  Pallas kernels: 37.7 us -> 27.5 us
  starting transfers between devices: 15.4 us -> 12.4 us
  waiting for transfers between devices: 26.3 us -> 29 us
    pallas_call x3, Pallas kernels: 15.3 us -> 6.62 us  [project(): pl.pallas_call(functools.partial(project_kernel, len(parts), len(added),...]
    ppermute x1, waiting for transfers between devices: 0.01 us -> 2.97 us  [per_device(): got = lax.ppermute(shares[2], 'head', hops[1])]
    ppermute x6 -> x4, starting transfers between devices: 4.78 us -> 2.75 us  [the longest x1 1.65 us: per_device(): lax.ppermute(other, 'ctx', far)]
    pallas_call x6, Pallas kernels: 21.6 us -> 20 us  [the longest x2 15 us: attend(): pl.pallas_call(functools.partial(attention_kernel, key_blocks, query_bloc...]
    ppermute x6 -> x4, waiting for transfers between devices: 6.86 us -> 8.12 us  [the longest x1 8.06 us: per_device(): lax.ppermute(own, 'ctx', far)]
    ppermute x3, waiting for transfers between devices: 7.9 us -> 6.87 us  [per_device(): lax.ppermute(shares[d], 'head', hops[d])]
    ppermute x1, waiting for transfers between devices: 6.69 us -> 5.69 us  [per_device(): chunks.append([shares[0], got, lax.ppermute(away, 'head', hops[2])])]
    ppermute x1, starting transfers between devices: 1.77 us -> 0.81 us  [per_device(): chunks.append([shares[0], got, lax.ppermute(away, 'head', hops[2])])]
  transfers between devices with their start and end apart: 13 -> 11, of which waited for: 7 -> 8; matrix products, arithmetic and copies ran while one was open for 1% -> 0% of each run, Pallas kernels for 28% -> 21%
where the time goes in v1:
time: 68.4 us; the launch traced here: 69 us
  waiting for transfers between devices  29 us (42%)
  Pallas kernels  27.5 us (40%)
  starting transfers between devices  12.4 us (18%)
    pallas_call x2, Pallas kernels, attend(): pl.pallas_call(functools.partial(attention_kernel, key_blocks, query_bloc...  15 us
    ppermute x1, waiting for transfers between devices, per_device(): lax.ppermute(own, 'ctx', far)  8.06 us
    ppermute x3, waiting for transfers between devices, per_device(): lax.ppermute(shares[d], 'head', hops[d])  6.87 us
    pallas_call x3, Pallas kernels, project(): pl.pallas_call(functools.partial(project_kernel, len(parts), len(added),...  6.62 us
    ppermute x1, waiting for transfers between devices, per_device(): chunks.append([shares[0], got, lax.ppermute(away, 'head', hops[2])])  5.69 us
    ppermute x3, starting transfers between devices, per_device(): lax.ppermute(shares[d], 'head', hops[d])  4.45 us
    ppermute x1, waiting for transfers between devices, per_device(): got = lax.ppermute(shares[2], 'head', hops[1])  2.97 us
    ppermute x1, waiting for transfers between devices, per_device(): q_far = lax.ppermute(q_mine, 'ctx', far)  2.94 us
  transfers between devices with their start and end apart: 11, of which 8 were waited for; matrix products, arithmetic and copies ran while one was open for 0% of the time, Pallas kernels for 21%

profile of v1, /device:TPU:0, one launch (start us, length us, event | category | flops | bytes accessed | tf_op | source)
XLA Modules:
  0.0 69.0 jit_solution(2110024116331429873)
XLA Ops:
  0.0 1.4 %pack.3 = bf16[4672,128]{1,0:T(8,128)(2,1)S(1)} custom-call(bf16[2048,256]{1,0:T(8,128)(2,1)} %refs_0_.3, bf16[2048,256]{1,0:T(8,128)(2,1)} %refs_1_.3, bf16[32,256]{1,0:T(8,128)(2,1)} %refs_2_.3, bf16[32,256]{1,0:T(8,128)(2,1)} %refs_3_.3, bf16[32,4096]{1,0:T(8,128)(2,1)} %q_ref.1), custom_call_target="tpu_custom_call" | custom-call | tf_op jit(solution)/shard_map/pack/pallas_call | solution.py:57
  1.4 0.5 collective-permute-start
  1.9 1.0 %split.1 = (bf16[32,2048]{1,0:T(8,128)(2,1)S(1)}, bf16[32,2048]{1,0:T(8,128)(2,1)S(1)}) custom-call(bf16[32,4096]{1,0:T(8,128)(2,1)} %q_ref.1), custom_call_target="tpu_custom_call" | custom-call | tf_op jit(solution)/shard_map/split/pallas_call | solution.py:83
  2.9 2.6 %collective-permute-start.1 = (bf16[32,2048]{1,0:T(8,128)(2,1)S(1)}, bf16[32,2048]{1,0:T(8,128)(2,1)S(1)}, u32[]{:S(2)}, u32[]{:S(2)}) collective-permute-start(bf16[32,2048]{1,0:T(8,128)(2,1)S(1)} %get-tuple-element.20.rest_2_), channel_id=1, source_target_pairs={{0,8},{4,12},{8,0},{12,4},{1,9},{5,13},{9,1},{13,5},{2,10},{6,14},... | collective-permute-start | bytes 393224 | tf_op jit(solution)/shard_map/ppermute | solution.py:457
  5.5 0.2 collective-permute-start.2
  5.7 1.2 %pack.2.rest_0_ = bf16[4160,128]{1,0:T(8,128)(2,1)S(1)} custom-call(bf16[2048,256]{1,0:T(8,128)(2,1)} %refs_0_.3, bf16[2048,256]{1,0:T(8,128)(2,1)} %refs_1_.3, bf16[32,256]{1,0:T(8,128)(2,1)} %refs_2_.3, bf16[32,256]{1,0:T(8,128)(2,1)} %refs_3_.3), custom_call_target="tpu_custom_call" | custom-call | tf_op jit(solution)/shard_map/pack/pallas_call | solution.py:57
  6.9 2.9 %collective-permute-done.1.rest_2_ = bf16[32,2048]{1,0:T(8,128)(2,1)S(1)} collective-permute-done((bf16[32,2048]{1,0:T(8,128)(2,1)S(1)}, bf16[32,2048]{1,0:T(8,128)(2,1)S(1)}, u32[]{:S(2)}, u32[]{:S(2)}) %collective-permute-start.1) | collective-permute-done | bytes 131104 | tf_op jit(solution)/shard_map/ppermute | solution.py:457
  9.9 2.4 %collective-permute-done.2.rest_3_ = bf16[32,2048]{1,0:T(8,128)(2,1)S(1)} collective-permute-done((bf16[32,2048]{1,0:T(8,128)(2,1)S(1)}, bf16[32,2048]{1,0:T(8,128)(2,1)S(1)}, u32[]{:S(2)}, u32[]{:S(2)}) %collective-permute-start.2) | collective-permute-done | bytes 131104 | tf_op jit(solution)/shard_map/ppermute | solution.py:458
  12.3 0.0 collective-permute-done.rest_1_
  12.3 7.5 %attend.3 = (bf16[64,2176]{1,0:T(8,128)(2,1)S(1)}, bf16[2048,2048]{1,0:T(8,128)(2,1)S(1)}, bf16[2048,2048]{1,0:T(8,128)(2,1)S(1)}) custom-call(s32[4,4]{1,0:T(4,128)} %new_ref.3, s32[4,4]{1,0:T(4,128)} %cache_ref.3, bf16[4096,4096]{1,0:T(8,128)(2,1)} %weight_ref.3, bf16[4160,128]{1,0:T(8,128)(2,1)S(1)} %pack.2.rest_0_, ...), custom_call_target="tpu_custom_call" | custom-call | flops 1937768448 | bytes 16777216 | tf_op jit(solution)/shard_map/attend/pallas_call | solution.py:278
  19.8 0.0 copy-start
  19.8 1.7 %collective-permute-start.3 = (bf16[64,2176]{1,0:T(8,128)(2,1)S(1)}, bf16[64,2176]{1,0:T(8,128)(2,1)S(1)}, u32[]{:S(2)}, u32[]{:S(2)}) collective-permute-start(bf16[64,2176]{1,0:T(8,128)(2,1)S(1)} %get-tuple-element.23.refs_2_), channel_id=1, source_target_pairs={{0,8},{4,12},{8,0},{12,4},{1,9},{5,13},{9,1},{13,5},{2,10},{6,14},... | collective-permute-start | bytes 835592 | tf_op jit(solution)/shard_map/ppermute | solution.py:499
  21.5 7.5 %attend.2 = (bf16[64,2176]{1,0:T(8,128)(2,1)S(1)}, bf16[2048,2048]{1,0:T(8,128)(2,1)S(1)}, bf16[2048,2048]{1,0:T(8,128)(2,1)S(1)}) custom-call(s32[4,4]{1,0:T(4,128)} %new_ref.3, s32[4,4]{1,0:T(4,128)} %cache_ref.3, bf16[4096,4096]{1,0:T(8,128)(2,1)} %weight_ref.3, bf16[4160,128]{1,0:T(8,128)(2,1)S(1)} %pack.2.rest_0_, ...), custom_call_target="tpu_custom_call" | custom-call | flops 1937768448 | bytes 16777216 | tf_op jit(solution)/shard_map/attend/pallas_call | solution.py:278
  29.0 0.5 collective-permute-start.4
  29.5 0.0 collective-permute-done.3.refs_1_
  29.5 8.1 %collective-permute-done.4.refs_3_ = bf16[64,2176]{1,0:T(8,128)(2,1)S(1)} collective-permute-done((bf16[64,2176]{1,0:T(8,128)(2,1)S(1)}, bf16[64,2176]{1,0:T(8,128)(2,1)S(1)}, u32[]{:S(2)}, u32[]{:S(2)}) %collective-permute-start.4) | collective-permute-done | bytes 278560 | tf_op jit(solution)/shard_map/ppermute | solution.py:499
  37.6 0.0 copy-done
  37.6 1.4 %combine.1.refs_0_ = bf16[128,2048]{1,0:T(8,128)(2,1)S(1)} custom-call(s32[128]{0:T(128)S(1)} %copy-done, bf16[64,2176]{1,0:T(8,128)(2,1)S(1)} %get-tuple-element.21.refs_0_, bf16[64,2176]{1,0:T(8,128)(2,1)S(1)} %collective-permute-done.3.refs_1_, bf16[64,2176]{1,0:T(8,128)(2,1)S(1)} %get-tuple-element.23.refs_2_, ...), custom_call_target="tpu_custom_call" | custom-call | tf_op jit(solution)/shard_map/combine/pallas_call | solution.py:355
  38.9 0.1 collective-permute-start.5
  39.0 1.8 %project.3.refs_2_ = f32[128,2048]{1,0:T(8,128)S(1)} custom-call(bf16[128,2048]{1,0:T(8,128)(2,1)S(1)} %combine.1.refs_0_, bf16[2048,2048]{1,0:T(8,128)(2,1)S(1)} %get-tuple-element.25.refs_1_), custom_call_target="tpu_custom_call" | custom-call | flops 2147483648 | bytes 4194304 | tf_op jit(solution)/shard_map/project/pallas_call | solution.py:387
  40.9 0.1 collective-permute-done.5.refs_0_.refs_1_
  40.9 1.9 %project.4 = (f32[32,2048]{1,0:T(8,128)S(1)}, f32[32,2048]{1,0:T(8,128)S(1)}, bf16[64,2048]{1,0:T(8,128)(2,1)S(1)}) custom-call(bf16[128,2048]{1,0:T(8,128)(2,1)S(1)} %collective-permute-done.5.refs_0_.refs_1_, bf16[2048,2048]{1,0:T(8,128)(2,1)S(1)} %get-tuple-element.24.refs_1_, f32[128,2048]{1,0:T(8,128)S(1)} %project.3.refs_2_), custom_call_target="tpu_custom_call" | custom-call | flops 2147483648 | bytes 4194304 | tf_op jit(solution)/shard_map/project/pallas_call | solution.py:387
  42.8 1.6 %collective-permute-start.6 = (bf16[64,2048]{1,0:T(8,128)(2,1)S(1)}, bf16[64,2048]{1,0:T(8,128)(2,1)S(1)}, u32[]{:S(2)}, u32[]{:S(2)}) collective-permute-start(bf16[64,2048]{1,0:T(8,128)(2,1)S(1)} %get-tuple-element.27), channel_id=1, source_target_pairs={{0,1},{1,0},{2,3},{3,2},{4,5},{5,4},{6,7},{7,6},{8,9},{9,8},{10,11... | collective-permute-start | bytes 786440 | tf_op jit(solution)/shard_map/ppermute | solution.py:547
  44.4 2.9 %project.5 = (f32[32,2048]{1,0:T(8,128)S(1)}, bf16[32,2048]{1,0:T(8,128)(2,1)S(1)}, bf16[32,2048]{1,0:T(8,128)(2,1)S(1)}, bf16[32,2048]{1,0:T(8,128)(2,1)S(1)}) custom-call(bf16[128,2048]{1,0:T(8,128)(2,1)S(1)} %combine.1.refs_0_, bf16[128,2048]{1,0:T(8,128)(2,1)S(1)} %collective-permute-done.5.refs_0_.refs_1_, ...), custom_call_target="tpu_custom_call" | custom-call | flops 4294967296 | bytes 8388608 | tf_op jit(solution)/shard_map/project/pallas_call | solution.py:387
  47.3 0.5 collective-permute-start.8
  47.9 2.6 %collective-permute-start.9 = (bf16[32,2048]{1,0:T(8,128)(2,1)S(1)}, bf16[32,2048]{1,0:T(8,128)(2,1)S(1)}, u32[]{:S(2)}, u32[]{:S(2)}) collective-permute-start(bf16[32,2048]{1,0:T(8,128)(2,1)S(1)} %get-tuple-element.33), channel_id=1, source_target_pairs={{0,2},{1,3},{2,0},{3,1},{4,6},{5,7},{6,4},{7,5},{8,10},{9,11},{10,... | collective-permute-start | bytes 393224 | tf_op jit(solution)/shard_map/ppermute | solution.py:554
  50.4 1.3 %collective-permute-start.10 = (bf16[32,2048]{1,0:T(8,128)(2,1)S(1)}, bf16[32,2048]{1,0:T(8,128)(2,1)S(1)}, u32[]{:S(2)}, u32[]{:S(2)}) collective-permute-start(bf16[32,2048]{1,0:T(8,128)(2,1)S(1)} %get-tuple-element.34), channel_id=1, source_target_pairs={{0,3},{1,2},{2,1},{3,0},{4,7},{5,6},{6,5},{7,4},{8,11},{9,10},{10,... | collective-permute-start | bytes 393224 | tf_op jit(solution)/shard_map/ppermute | solution.py:554
  51.8 3.0 %collective-permute-done.6.refs_1_ = bf16[64,2048]{1,0:T(8,128)(2,1)S(1)} collective-permute-done((bf16[64,2048]{1,0:T(8,128)(2,1)S(1)}, bf16[64,2048]{1,0:T(8,128)(2,1)S(1)}, u32[]{:S(2)}, u32[]{:S(2)}) %collective-permute-start.6) | collective-permute-done | bytes 262176 | tf_op jit(solution)/shard_map/ppermute | solution.py:547
  54.8 0.8 %collective-permute-start.7 = (bf16[32,2048]{1,0:T(8,128)(2,1)S(1)}, bf16[32,2048]{1,0:T(8,128)(2,1)S(1)}, u32[]{:S(2)}, u32[]{:S(2)}) collective-permute-start(bf16[32,2048]{1,0:T(8,128)(2,1)S(1)} %add_convert_fusion), channel_id=1, source_target_pairs={{0,2},{1,3},{2,0},{3,1},{4,6},{5,7},{6,4},{7,5},{8,10},{9,11},{10,... | collective-permute-start | bytes 393224 | tf_op jit(solution)/shard_map/ppermute | solution.py:549
  55.6 1.7 %collective-permute-done.8.refs_4_ = bf16[32,2048]{1,0:T(8,128)(2,1)S(1)} collective-permute-done((bf16[32,2048]{1,0:T(8,128)(2,1)S(1)}, bf16[32,2048]{1,0:T(8,128)(2,1)S(1)}, u32[]{:S(2)}, u32[]{:S(2)}) %collective-permute-start.8) | collective-permute-done | bytes 131104 | tf_op jit(solution)/shard_map/ppermute | solution.py:554
  57.3 0.0 collective-permute-done.9.refs_5_
  57.3 5.1 %collective-permute-done.10.refs_6_ = bf16[32,2048]{1,0:T(8,128)(2,1)S(1)} collective-permute-done((bf16[32,2048]{1,0:T(8,128)(2,1)S(1)}, bf16[32,2048]{1,0:T(8,128)(2,1)S(1)}, u32[]{:S(2)}, u32[]{:S(2)}) %collective-permute-start.10) | collective-permute-done | bytes 131104 | tf_op jit(solution)/shard_map/ppermute | solution.py:554
  62.5 5.7 %collective-permute-done.7.refs_2_ = bf16[32,2048]{1,0:T(8,128)(2,1)S(1)} collective-permute-done((bf16[32,2048]{1,0:T(8,128)(2,1)S(1)}, bf16[32,2048]{1,0:T(8,128)(2,1)S(1)}, u32[]{:S(2)}, u32[]{:S(2)}) %collective-permute-start.7) | collective-permute-done | bytes 131104 | tf_op jit(solution)/shard_map/ppermute | solution.py:549
  68.2 0.8 %finish.1 = bf16[32,4096]{1,0:T(8,128)(2,1)} custom-call(f32[32,2048]{1,0:T(8,128)S(1)} %get-tuple-element.26.refs_0_, bf16[64,2048]{1,0:T(8,128)(2,1)S(1)} %collective-permute-done.6.refs_1_, bf16[32,2048]{1,0:T(8,128)(2,1)S(1)} %collective-permute-done.7.refs_2_, f32[32,2048]{1,0:T(8,128)S(1)} %get-tuple-element.31.refs_3_, ...), custom_call_target="tpu_custom_call" | custom-call | tf_op jit(solution)/shard_map/finish/pallas_call | solution.py:419
  (1 shorter events, 0.0 us)
Async XLA Ops:
  1.4 10.9 %collective-permute-start = (bf16[4672,128]{1,0:T(8,128)(2,1)S(1)}, bf16[4672,128]{1,0:T(8,128)(2,1)S(1)}, u32[]{:S(2)}, u32[]{:S(2)}) collective-permute-start(bf16[4672,128]{1,0:T(8,128)(2,1)S(1)} %pack.3), channel_id=1, source_target_pairs={{0,4},{4,0},{8,12},{12,8},{1,5},{5,1},{9,13},{13,9},{2,6},{6,2},{1... | collective-permute-start | bytes 3588104 | tf_op jit(solution)/shard_map/ppermute | solution.py:462
  2.9 7.0 %collective-permute-start.1 = (bf16[32,2048]{1,0:T(8,128)(2,1)S(1)}, bf16[32,2048]{1,0:T(8,128)(2,1)S(1)}, u32[]{:S(2)}, u32[]{:S(2)}) collective-permute-start(bf16[32,2048]{1,0:T(8,128)(2,1)S(1)} %get-tuple-element.20.rest_2_), channel_id=1, source_target_pairs={{0,8},{4,12},{8,0},{12,4},{1,9},{5,13},{9,1},{13,5},{2,10},{6,14},... | collective-permute-start | bytes 393224 | tf_op jit(solution)/shard_map/ppermute | solution.py:457
  5.5 6.7 %collective-permute-start.2 = (bf16[32,2048]{1,0:T(8,128)(2,1)S(1)}, bf16[32,2048]{1,0:T(8,128)(2,1)S(1)}, u32[]{:S(2)}, u32[]{:S(2)}) collective-permute-start(bf16[32,2048]{1,0:T(8,128)(2,1)S(1)} %get-tuple-element.22), channel_id=1, source_target_pairs={{0,12},{4,8},{8,4},{12,0},{1,13},{5,9},{9,5},{13,1},{2,14},{6,10},... | collective-permute-start | bytes 393224 | tf_op jit(solution)/shard_map/ppermute | solution.py:458
  19.8 17.8 %copy-start = (s32[128]{0:T(128)S(1)}, s32[128]{0:T(128)}, u32[]{:S(2)}) copy-start(s32[128]{0:T(128)} %dest_ref.1) | copy-start | bytes 1540
  19.8 9.7 %collective-permute-start.3 = (bf16[64,2176]{1,0:T(8,128)(2,1)S(1)}, bf16[64,2176]{1,0:T(8,128)(2,1)S(1)}, u32[]{:S(2)}, u32[]{:S(2)}) collective-permute-start(bf16[64,2176]{1,0:T(8,128)(2,1)S(1)} %get-tuple-element.23.refs_2_), channel_id=1, source_target_pairs={{0,8},{4,12},{8,0},{12,4},{1,9},{5,13},{9,1},{13,5},{2,10},{6,14},... | collective-permute-start | bytes 835592 | tf_op jit(solution)/shard_map/ppermute | solution.py:499
  29.0 8.6 %collective-permute-start.4 = (bf16[64,2176]{1,0:T(8,128)(2,1)S(1)}, bf16[64,2176]{1,0:T(8,128)(2,1)S(1)}, u32[]{:S(2)}, u32[]{:S(2)}) collective-permute-start(bf16[64,2176]{1,0:T(8,128)(2,1)S(1)} %get-tuple-element.21.refs_0_), channel_id=1, source_target_pairs={{0,8},{4,12},{8,0},{12,4},{1,9},{5,13},{9,1},{13,5},{2,10},{6,14},... | collective-permute-start | bytes 835592 | tf_op jit(solution)/shard_map/ppermute | solution.py:499
  38.9 2.0 %collective-permute-start.5 = (bf16[128,2048]{1,0:T(8,128)(2,1)S(1)}, bf16[128,2048]{1,0:T(8,128)(2,1)S(1)}, u32[]{:S(2)}, u32[]{:S(2)}) collective-permute-start(bf16[128,2048]{1,0:T(8,128)(2,1)S(1)} %combine.1.refs_0_), channel_id=1, source_target_pairs={{0,4},{4,0},{8,12},{12,8},{1,5},{5,1},{9,13},{13,9},{2,6},{6,2},{1... | collective-permute-start | bytes 1572872 | tf_op jit(solution)/shard_map/ppermute | solution.py:501
  42.8 12.0 %collective-permute-start.6 = (bf16[64,2048]{1,0:T(8,128)(2,1)S(1)}, bf16[64,2048]{1,0:T(8,128)(2,1)S(1)}, u32[]{:S(2)}, u32[]{:S(2)}) collective-permute-start(bf16[64,2048]{1,0:T(8,128)(2,1)S(1)} %get-tuple-element.27), channel_id=1, source_target_pairs={{0,1},{1,0},{2,3},{3,2},{4,5},{5,4},{6,7},{7,6},{8,9},{9,8},{10,11... | collective-permute-start | bytes 786440 | tf_op jit(solution)/shard_map/ppermute | solution.py:547
  47.3 10.0 %collective-permute-start.8 = (bf16[32,2048]{1,0:T(8,128)(2,1)S(1)}, bf16[32,2048]{1,0:T(8,128)(2,1)S(1)}, u32[]{:S(2)}, u32[]{:S(2)}) collective-permute-start(bf16[32,2048]{1,0:T(8,128)(2,1)S(1)} %get-tuple-element.32), channel_id=1, source_target_pairs={{0,1},{1,0},{2,3},{3,2},{4,5},{5,4},{6,7},{7,6},{8,9},{9,8},{10,11... | collective-permute-start | bytes 393224 | tf_op jit(solution)/shard_map/ppermute | solution.py:554
  47.9 9.5 %collective-permute-start.9 = (bf16[32,2048]{1,0:T(8,128)(2,1)S(1)}, bf16[32,2048]{1,0:T(8,128)(2,1)S(1)}, u32[]{:S(2)}, u32[]{:S(2)}) collective-permute-start(bf16[32,2048]{1,0:T(8,128)(2,1)S(1)} %get-tuple-element.33), channel_id=1, source_target_pairs={{0,2},{1,3},{2,0},{3,1},{4,6},{5,7},{6,4},{7,5},{8,10},{9,11},{10,... | collective-permute-start | bytes 393224 | tf_op jit(solution)/shard_map/ppermute | solution.py:554
  50.4 12.0 %collective-permute-start.10 = (bf16[32,2048]{1,0:T(8,128)(2,1)S(1)}, bf16[32,2048]{1,0:T(8,128)(2,1)S(1)}, u32[]{:S(2)}, u32[]{:S(2)}) collective-permute-start(bf16[32,2048]{1,0:T(8,128)(2,1)S(1)} %get-tuple-element.34), channel_id=1, source_target_pairs={{0,3},{1,2},{2,1},{3,0},{4,7},{5,6},{6,5},{7,4},{8,11},{9,10},{10,... | collective-permute-start | bytes 393224 | tf_op jit(solution)/shard_map/ppermute | solution.py:554
  54.8 13.4 %collective-permute-start.7 = (bf16[32,2048]{1,0:T(8,128)(2,1)S(1)}, bf16[32,2048]{1,0:T(8,128)(2,1)S(1)}, u32[]{:S(2)}, u32[]{:S(2)}) collective-permute-start(bf16[32,2048]{1,0:T(8,128)(2,1)S(1)} %add_convert_fusion), channel_id=1, source_target_pairs={{0,2},{1,3},{2,0},{3,1},{4,6},{5,7},{6,4},{7,5},{8,10},{9,11},{10,... | collective-permute-start | bytes 393224 | tf_op jit(solution)/shard_map/ppermute | solution.py:549

commit v2 on v1

--- a/solution.py
+++ b/solution.py
@@ -12,11 +12,18 @@
 CAPR = 512
 ROWS = 16
 ALIGN = 16
+CHAINS = 2
 NEG = -1e30
 SCALE = 1.0 / math.sqrt(HEAD_DIM)
 LOG2E = math.log2(math.e)
 SPANS = 2
 COPIES = 4
+
+
+def moves(*arrays):
+    return pl.CostEstimate(
+        flops=0, bytes_accessed=sum(2 * a.size * a.dtype.itemsize for a in arrays), transcendentals=0
+    )
 
 
 def in_hbm(a):
@@ -41,8 +48,8 @@
         rows = ref.shape[0]
         heads = (out_ref.shape[0] - at) // rows
         for g in range(heads):
-            columns = pl.ds(pl.multiple_of((block * heads + g) * HEAD_DIM, HEAD_DIM), HEAD_DIM)
-            copies.append((ref.at[:, columns], out_ref.at[at : at + rows, :]))
+            first = (number * heads + g) * HEAD_DIM
+            copies.append((ref.at[:, first : first + HEAD_DIM], out_ref.at[at : at + rows, :]))
             at += rows
     copies = [pltpu.make_async_copy(a, b, sems.at[n]) for n, (a, b) in enumerate(copies)]
     for c in copies:
@@ -52,17 +59,19 @@
 
 
 def pack(other, arrays, queries, kv, number):
-    group = queries[0].shape[1] // arrays[0].shape[1] if queries else 0
+    group = queries[0].shape[1] // HEAD_DIM // kv if queries else 0
     rows = sum(a.shape[0] for a in arrays) + sum(q.shape[0] * group for q in queries)
     return pl.pallas_call(
         functools.partial(pack_kernel, number, kv, other),
-        in_specs=[pl.BlockSpec(memory_space=pltpu.HBM)] * (len(arrays) + len(queries)),
+        in_specs=[pl.BlockSpec(memory_space=pltpu.HBM)] * len(arrays)
+        + [pl.BlockSpec(memory_space=pltpu.VMEM)] * len(queries),
         out_specs=pl.BlockSpec(memory_space=pltpu.VMEM),
         out_shape=jax.ShapeDtypeStruct((rows, HEAD_DIM), arrays[0].dtype),
         scratch_shapes=[pltpu.SemaphoreType.DMA((len(arrays) + group,))],
         compiler_params=pltpu.CompilerParams(vmem_limit_bytes=4 * 2**20),
+        cost_estimate=moves(jax.ShapeDtypeStruct((rows, HEAD_DIM), arrays[0].dtype)),
         name="pack",
-    )(*[in_hbm(a) for a in (*arrays, *queries)])
+    )(*[in_hbm(a) for a in arrays], *queries)
 
 
 def split_kernel(q_ref, *refs):
@@ -87,6 +96,7 @@
         out_shape=[half, half],
         scratch_shapes=[pltpu.SemaphoreType.DMA((2,))],
         compiler_params=pltpu.CompilerParams(vmem_limit_bytes=2 * 2**20),
+        cost_estimate=moves(a),
         name="split",
     )(in_hbm(a))
 
@@ -206,16 +216,6 @@
         ks = jnp.concatenate(ks, axis=0)
         vs = jnp.concatenate(vs, axis=0)
         row0 = pl.multiple_of(i * ROWS, ROWS)
-        q = jnp.concatenate(
-            [
-                sorted_q[pl.ds(row0, ROWS), g * HEAD_DIM : (g + 1) * HEAD_DIM]
-                for g in range(group)
-            ],
-            axis=0,
-        )
-        scores = lax.dot_general(
-            q, ks, (((1,), (1,)), ((), ())), preferred_element_type=jnp.float32
-        )
         bias = jnp.where(inside, 0.0, NEG)
         t = jnp.zeros((ROWS, 1), jnp.int32)
         among = (i - start_tile) * ROWS + lax.broadcasted_iota(jnp.int32, (ROWS, 1), 0)
@@ -227,25 +227,31 @@
             t = jnp.where(among >= base, block * block_rows + begin + among - base, t)
             base = base + new_counts(block, r)
         causal = jnp.where(key_pos[:, plain:] <= t, bias[:, plain:], NEG)
-        causal = jnp.concatenate([causal] * group, axis=0)
-        scores = jnp.concatenate(
-            [scores[:, :plain] + bias[:, :plain], scores[:, plain:] + causal], axis=1
-        )
-        top = jnp.max(scores, axis=1, keepdims=True)
-        probs = jnp.exp2((scores - top) * (SCALE * LOG2E)).astype(jnp.bfloat16)
-        mixed = jnp.dot(
-            probs,
-            jnp.concatenate([vs, ones], axis=1),
-            preferred_element_type=jnp.float32,
-        )
-        total = mixed[:, HEAD_DIM:]
-        value = (mixed[:, :HEAD_DIM] / total).astype(jnp.bfloat16)
-        lse = top * SCALE + jnp.log(total)
+        values = jnp.concatenate([vs, ones], axis=1)
         logs = jnp.zeros((ROWS, 128), jnp.float32)
-        for g in range(group):
-            rows = slice(g * ROWS, (g + 1) * ROWS)
-            part[pl.ds(row0, ROWS), g * HEAD_DIM : (g + 1) * HEAD_DIM] = value[rows]
-            logs = jnp.where(lax.rem(lane, group) == g, lse[rows], logs)
+        together = group // CHAINS if group % CHAINS == 0 else group
+        causal = jnp.concatenate([causal] * together, axis=0)
+        for chain in range(0, group, together):
+            heads = range(chain, chain + together)
+            q = jnp.concatenate(
+                [sorted_q[pl.ds(row0, ROWS), g * HEAD_DIM : (g + 1) * HEAD_DIM] for g in heads], axis=0
+            )
+            scores = lax.dot_general(
+                q, ks, (((1,), (1,)), ((), ())), preferred_element_type=jnp.float32
+            )
+            scores = jnp.concatenate(
+                [scores[:, :plain] + bias[:, :plain], scores[:, plain:] + causal], axis=1
+            )
+            top = jnp.max(scores, axis=1, keepdims=True)
+            probs = jnp.exp2((scores - top) * (SCALE * LOG2E)).astype(jnp.bfloat16)
+            mixed = jnp.dot(probs, values, preferred_element_type=jnp.float32)
+            total = mixed[:, HEAD_DIM:]
+            value = (mixed[:, :HEAD_DIM] / total).astype(jnp.bfloat16)
+            lse = top * SCALE + jnp.log(total)
+            for n, g in enumerate(heads):
+                rows = slice(n * ROWS, (n + 1) * ROWS)
+                part[pl.ds(row0, ROWS), g * HEAD_DIM : (g + 1) * HEAD_DIM] = value[rows]
+                logs = jnp.where(lax.rem(lane, group) == g, lse[rows], logs)
         high = logs.astype(jnp.bfloat16)
         rest_of = logs - high.astype(jnp.float32)
         middle = rest_of.astype(jnp.bfloat16)
@@ -320,47 +326,76 @@
     return head * out_rows + lax.rem(dest, out_rows)
 
 
-def combine_kernel(group, heads, dest_ref, *refs):
-    sources, out_ref, gathered = refs[:-2], refs[-2], refs[-1]
+def mixed_head(a_ref, b_ref, g, weights):
+    at = slice(g * HEAD_DIM, (g + 1) * HEAD_DIM)
+    one = weights[0][:, g : g + 1] * a_ref[:, at].astype(jnp.float32)
+    one = one + weights[1][:, g : g + 1] * b_ref[:, at].astype(jnp.float32)
+    return one.astype(jnp.bfloat16)
+
+
+def mixing_weights(a_ref, b_ref, group):
+    cols = group * HEAD_DIM
+    sa, sb = log_sums(a_ref[:, cols:], group), log_sums(b_ref[:, cols:], group)
+    best = jnp.maximum(sa, sb)
+    wa, wb = jnp.exp(sa - best), jnp.exp(sb - best)
+    whole = wa + wb
+    return wa / whole, wb / whole
+
+
+def mix_kernel(group, a_ref, b_ref, out_ref):
+    weights = mixing_weights(a_ref, b_ref, group)
+    for g in range(group):
+        out_ref[:, g * HEAD_DIM : (g + 1) * HEAD_DIM] = mixed_head(a_ref, b_ref, g, weights)
+
+
+def mix(a, b):
+    vmem = pl.BlockSpec(memory_space=pltpu.VMEM)
+    cols = a.shape[1] - 128
+    return pl.pallas_call(
+        functools.partial(mix_kernel, cols // HEAD_DIM),
+        in_specs=[vmem] * 2,
+        out_specs=vmem,
+        out_shape=jax.ShapeDtypeStruct((a.shape[0], cols), jnp.bfloat16),
+        compiler_params=pltpu.CompilerParams(vmem_limit_bytes=4 * 2**20),
+        cost_estimate=moves(a, b),
+        name="mix",
+    )(a, b)
+
+
+def combine_kernel(group, heads, dest_ref, a_ref, b_ref, far_ref, out_ref, gathered):
     rows = out_ref.shape[0]
-    cols = group * HEAD_DIM
+    half_rows = a_ref.shape[0]
+    block_rows = half_rows // 2
     me = lax.axis_index("ctx")
-    blocks = len(sources)
-    block_rows = rows // blocks
-    for n in range(0, blocks, 2):
-        a_ref, b_ref = sources[n], sources[n + 1]
-        sa, sb = log_sums(a_ref[:, cols:], group), log_sums(b_ref[:, cols:], group)
-        best = jnp.maximum(sa, sb)
-        wa, wb = jnp.exp(sa - best), jnp.exp(sb - best)
-        whole = wa + wb
-        wa, wb = wa / whole, wb / whole
-        for g in range(group):
-            at = slice(g * HEAD_DIM, (g + 1) * HEAD_DIM)
-            one = wa[:, g : g + 1] * a_ref[:, at].astype(jnp.float32)
-            one = one + wb[:, g : g + 1] * b_ref[:, at].astype(jnp.float32)
-            one = one.astype(jnp.bfloat16)
-            for k in range(2):
-                first = pl.multiple_of((me ^ (n + k)) * block_rows, ALIGN)
-                gathered[pl.ds(first, block_rows), at] = one[k * block_rows : (k + 1) * block_rows]
+    weights = mixing_weights(a_ref, b_ref, group)
     dest = places(dest_ref[...].reshape(1, rows), rows // heads, heads)
     landing = (lax.broadcasted_iota(jnp.int32, (rows, rows), 0) == dest).astype(jnp.bfloat16)
+    first = [pl.multiple_of((me ^ n) * block_rows, ALIGN) for n in range(4)]
+    for g in range(group):
+        at = slice(g * HEAD_DIM, (g + 1) * HEAD_DIM)
+        one = mixed_head(a_ref, b_ref, g, weights)
+        for k in range(2):
+            here = slice(k * block_rows, (k + 1) * block_rows)
+            gathered[pl.ds(first[k], block_rows), at] = one[here]
+            gathered[pl.ds(first[2 + k], block_rows), at] = far_ref[here, at]
     out_ref[...] = jnp.dot(landing, gathered[...], preferred_element_type=jnp.float32).astype(
         jnp.bfloat16
     )
 
 
-def combine(dest, arrays, heads):
+def combine(dest, a, b, far, heads):
     vmem = pl.BlockSpec(memory_space=pltpu.VMEM)
-    cols = arrays[0].shape[1] - 128
+    cols = far.shape[1]
     return pl.pallas_call(
         functools.partial(combine_kernel, cols // HEAD_DIM, heads),
-        in_specs=[vmem] * (1 + len(arrays)),
+        in_specs=[vmem] * 4,
         out_specs=vmem,
         out_shape=jax.ShapeDtypeStruct((dest.shape[0], cols), jnp.bfloat16),
         scratch_shapes=[pltpu.VMEM((dest.shape[0], cols), jnp.bfloat16)],
         compiler_params=pltpu.CompilerParams(vmem_limit_bytes=6 * 2**20),
+        cost_estimate=moves(a, b, far),
         name="combine",
-    )(dest, *arrays)
+    )(dest, a, b, far)
 
 
 def project_kernel(parts, added, cuts, step, *refs):
@@ -459,7 +494,7 @@
         packed = [
             [
                 pack(False, caches, [], kv, i),
-                lax.ppermute(pack(True, caches, [queries], kv, i), "ctx", near),
+                lax.ppermute(pack(True, caches, [q_other], kv, i), "ctx", near),
             ]
             for i in range(kv)
         ]
@@ -497,7 +532,7 @@
         for i in range(kv):
             own, other = results[i], results[kv + i]
             from_own, from_other = lax.ppermute(own, "ctx", far), lax.ppermute(other, "ctx", far)
-            mine.append(combine(row_dest, [own, from_other, other, from_own], heads))
+            mine.append(combine(row_dest, own, from_other, mix(other, from_own), heads))
         others = [lax.ppermute(a, "ctx", near) for a in mine]
     else:
         mine, others = [], []

time: 68.4 us -> 61.3 us (0.90); the launches traced: 69 us -> 61.1 us
  waiting for transfers between devices: 29 us -> 19.2 us
  starting transfers between devices: 12.4 us -> 16 us
  Pallas kernels: 27.5 us -> 25.8 us
    ppermute x1, waiting for transfers between devices: 8.06 us -> 0.01 us  [per_device(): lax.ppermute(own, 'ctx', far)]
    ppermute x1, waiting for transfers between devices: 0.01 us -> 7.56 us  [per_device(): lax.ppermute(other, 'ctx', far)]
    ppermute x1, starting transfers between devices: 0.81 us -> 4.43 us  [per_device(): chunks.append([shares[0], got, lax.ppermute(away, 'head', hops[2])])]
    ppermute x1, waiting for transfers between devices: 5.69 us -> 2.36 us  [per_device(): chunks.append([shares[0], got, lax.ppermute(away, 'head', hops[2])])]
    ppermute x1, waiting for transfers between devices: 2.97 us -> 0.01 us  [per_device(): got = lax.ppermute(shares[2], 'head', hops[1])]
    ppermute x1, waiting for transfers between devices: 2.94 us -> 0.01 us  [per_device(): q_far = lax.ppermute(q_mine, 'ctx', far)]
    ppermute x1, starting transfers between devices: 2.61 us -> 0.04 us  [per_device(): q_far = lax.ppermute(q_mine, 'ctx', far)]
    ppermute x1, starting transfers between devices: 0.16 us -> 2.64 us  [per_device(): q_across = lax.ppermute(q_other, 'ctx', across)]
  transfers between devices with their start and end apart: 11 -> 11, of which waited for: 8 -> 6; matrix products, arithmetic and copies ran while one was open for 0% -> 0% of each run, Pallas kernels for 21% -> 33%
where the time goes in v2:
time: 61.3 us; the launch traced here: 61.1 us
  Pallas kernels  25.8 us (42%)
  waiting for transfers between devices  19.2 us (31%)
  starting transfers between devices  16 us (26%)
    pallas_call x2, Pallas kernels, attend(): pl.pallas_call(functools.partial(attention_kernel, key_blocks, query_bloc...  13.5 us
    ppermute x3, waiting for transfers between devices, per_device(): lax.ppermute(shares[d], 'head', hops[d])  9.25 us
    ppermute x1, waiting for transfers between devices, per_device(): lax.ppermute(other, 'ctx', far)  7.56 us
    pallas_call x3, Pallas kernels, project(): pl.pallas_call(functools.partial(project_kernel, len(parts), len(added),...  6.63 us
    ppermute x3, starting transfers between devices, per_device(): lax.ppermute(shares[d], 'head', hops[d])  4.45 us
    ppermute x1, starting transfers between devices, per_device(): chunks.append([shares[0], got, lax.ppermute(away, 'head', hops[2])])  4.43 us
    pallas_call x2, Pallas kernels, pack(): pl.pallas_call(functools.partial(pack_kernel, number, kv, other), in_spec...  2.66 us
    ppermute x1, starting transfers between devices, per_device(): q_across = lax.ppermute(q_other, 'ctx', across)  2.64 us
  transfers between devices with their start and end apart: 11, of which 6 were waited for; matrix products, arithmetic and copies ran while one was open for 0% of the time, Pallas kernels for 33%

profile of v2, /device:TPU:0, one launch (start us, length us, event | category | flops | bytes accessed | tf_op | source)
XLA Modules:
  0.0 61.1 jit_solution(4220764919602621761)
XLA Ops:
  0.0 1.0 %split.1 = (bf16[32,2048]{1,0:T(8,128)(2,1)S(1)}, bf16[32,2048]{1,0:T(8,128)(2,1)S(1)}) custom-call(bf16[32,4096]{1,0:T(8,128)(2,1)} %q_ref.1), custom_call_target="tpu_custom_call" | custom-call | bytes 524288 | tf_op jit(solution)/shard_map/split/pallas_call | solution.py:92
  1.0 1.4 %pack.3 = bf16[4672,128]{1,0:T(8,128)(2,1)S(1)} custom-call(bf16[2048,256]{1,0:T(8,128)(2,1)} %refs_0_.3, bf16[2048,256]{1,0:T(8,128)(2,1)} %refs_1_.3, bf16[32,256]{1,0:T(8,128)(2,1)} %refs_2_.3, bf16[32,256]{1,0:T(8,128)(2,1)} %refs_3_.3, bf16[32,2048]{1,0:T(8,128)(2,1)S(1)} %get-tuple-element.20.refs_4_), custom_call_target="tpu_custom_call" | custom-call | bytes 2392064 | tf_op jit(solution)/shard_map/pack/pallas_call | solution.py:64
  2.4 0.5 collective-permute-start
  2.9 2.6 %collective-permute-start.2 = (bf16[32,2048]{1,0:T(8,128)(2,1)S(1)}, bf16[32,2048]{1,0:T(8,128)(2,1)S(1)}, u32[]{:S(2)}, u32[]{:S(2)}) collective-permute-start(bf16[32,2048]{1,0:T(8,128)(2,1)S(1)} %get-tuple-element.20.refs_4_), channel_id=1, source_target_pairs={{0,12},{4,8},{8,4},{12,0},{1,13},{5,9},{9,5},{13,1},{2,14},{6,10},... | collective-permute-start | bytes 393224 | tf_op jit(solution)/shard_map/ppermute | solution.py:493
  5.6 0.0 collective-permute-start.1
  5.6 1.2 %pack.2.rest_0_ = bf16[4160,128]{1,0:T(8,128)(2,1)S(1)} custom-call(bf16[2048,256]{1,0:T(8,128)(2,1)} %refs_0_.3, bf16[2048,256]{1,0:T(8,128)(2,1)} %refs_1_.3, bf16[32,256]{1,0:T(8,128)(2,1)} %refs_2_.3, bf16[32,256]{1,0:T(8,128)(2,1)} %refs_3_.3), custom_call_target="tpu_custom_call" | custom-call | bytes 2129920 | tf_op jit(solution)/shard_map/pack/pallas_call | solution.py:64
  6.9 0.0 collective-permute-done.rest_1_
  6.9 6.7 %attend.2 = (bf16[64,2176]{1,0:T(8,128)(2,1)S(1)}, bf16[2048,2048]{1,0:T(8,128)(2,1)S(1)}, bf16[2048,2048]{1,0:T(8,128)(2,1)S(1)}) custom-call(s32[4,4]{1,0:T(4,128)} %new_ref.3, s32[4,4]{1,0:T(4,128)} %cache_ref.3, bf16[4096,4096]{1,0:T(8,128)(2,1)} %weight_ref.3, bf16[4160,128]{1,0:T(8,128)(2,1)S(1)} %pack.2.rest_0_, ...), custom_call_target="tpu_custom_call" | custom-call | flops 1937768448 | bytes 16777216 | tf_op jit(solution)/shard_map/attend/pallas_call | solution.py:284
  13.6 0.0 copy-start
  13.6 2.0 %collective-permute-start.4 = (bf16[64,2176]{1,0:T(8,128)(2,1)S(1)}, bf16[64,2176]{1,0:T(8,128)(2,1)S(1)}, u32[]{:S(2)}, u32[]{:S(2)}) collective-permute-start(bf16[64,2176]{1,0:T(8,128)(2,1)S(1)} %get-tuple-element.22.a_ref), channel_id=1, source_target_pairs={{0,8},{4,12},{8,0},{12,4},{1,9},{5,13},{9,1},{13,5},{2,10},{6,14},... | collective-permute-start | bytes 835592 | tf_op jit(solution)/shard_map/ppermute | solution.py:534
  15.7 0.0 collective-permute-done.1.rest_2_
  15.7 0.0 collective-permute-done.2.rest_3_
  15.7 6.8 %attend.3 = (bf16[64,2176]{1,0:T(8,128)(2,1)S(1)}, bf16[2048,2048]{1,0:T(8,128)(2,1)S(1)}, bf16[2048,2048]{1,0:T(8,128)(2,1)S(1)}) custom-call(s32[4,4]{1,0:T(4,128)} %new_ref.3, s32[4,4]{1,0:T(4,128)} %cache_ref.3, bf16[4096,4096]{1,0:T(8,128)(2,1)} %weight_ref.3, bf16[4160,128]{1,0:T(8,128)(2,1)S(1)} %pack.2.rest_0_, ...), custom_call_target="tpu_custom_call" | custom-call | flops 1937768448 | bytes 16777216 | tf_op jit(solution)/shard_map/attend/pallas_call | solution.py:284
  22.4 0.1 collective-permute-start.3
  22.5 0.0 collective-permute-done.4.b_ref
  22.5 0.5 mix.1.far_ref
  23.0 7.6 %collective-permute-done.3.b_ref = bf16[64,2176]{1,0:T(8,128)(2,1)S(1)} collective-permute-done((bf16[64,2176]{1,0:T(8,128)(2,1)S(1)}, bf16[64,2176]{1,0:T(8,128)(2,1)S(1)}, u32[]{:S(2)}, u32[]{:S(2)}) %collective-permute-start.3) | collective-permute-done | bytes 278560 | tf_op jit(solution)/shard_map/ppermute | solution.py:534
  30.6 0.0 copy-done
  30.6 0.8 %combine.1.refs_0_ = bf16[128,2048]{1,0:T(8,128)(2,1)S(1)} custom-call(s32[128]{0:T(128)S(1)} %copy-done, bf16[64,2176]{1,0:T(8,128)(2,1)S(1)} %get-tuple-element.22.a_ref, bf16[64,2176]{1,0:T(8,128)(2,1)S(1)} %collective-permute-done.3.b_ref, bf16[64,2048]{1,0:T(8,128)(2,1)S(1)} %mix.1.far_ref), custom_call_target="tpu_custom_call" | custom-call | bytes 1638400 | tf_op jit(solution)/shard_map/combine/pallas_call | solution.py:389
  31.3 0.1 collective-permute-start.5
  31.4 1.8 %project.3.refs_2_ = f32[128,2048]{1,0:T(8,128)S(1)} custom-call(bf16[128,2048]{1,0:T(8,128)(2,1)S(1)} %combine.1.refs_0_, bf16[2048,2048]{1,0:T(8,128)(2,1)S(1)} %get-tuple-element.25.refs_1_), custom_call_target="tpu_custom_call" | custom-call | flops 2147483648 | bytes 4194304 | tf_op jit(solution)/shard_map/project/pallas_call | solution.py:422
  33.3 0.1 collective-permute-done.5.refs_0_.refs_1_
  33.3 1.9 %project.4 = (f32[32,2048]{1,0:T(8,128)S(1)}, f32[32,2048]{1,0:T(8,128)S(1)}, bf16[64,2048]{1,0:T(8,128)(2,1)S(1)}) custom-call(bf16[128,2048]{1,0:T(8,128)(2,1)S(1)} %collective-permute-done.5.refs_0_.refs_1_, bf16[2048,2048]{1,0:T(8,128)(2,1)S(1)} %get-tuple-element.24.refs_1_, f32[128,2048]{1,0:T(8,128)S(1)} %project.3.refs_2_), custom_call_target="tpu_custom_call" | custom-call | flops 2147483648 | bytes 4194304 | tf_op jit(solution)/shard_map/project/pallas_call | solution.py:422
  35.2 1.7 %collective-permute-start.6 = (bf16[64,2048]{1,0:T(8,128)(2,1)S(1)}, bf16[64,2048]{1,0:T(8,128)(2,1)S(1)}, u32[]{:S(2)}, u32[]{:S(2)}) collective-permute-start(bf16[64,2048]{1,0:T(8,128)(2,1)S(1)} %get-tuple-element.27), channel_id=1, source_target_pairs={{0,1},{1,0},{2,3},{3,2},{4,5},{5,4},{6,7},{7,6},{8,9},{9,8},{10,11... | collective-permute-start | bytes 786440 | tf_op jit(solution)/shard_map/ppermute | solution.py:582
  36.8 2.9 %project.5 = (f32[32,2048]{1,0:T(8,128)S(1)}, bf16[32,2048]{1,0:T(8,128)(2,1)S(1)}, bf16[32,2048]{1,0:T(8,128)(2,1)S(1)}, bf16[32,2048]{1,0:T(8,128)(2,1)S(1)}) custom-call(bf16[128,2048]{1,0:T(8,128)(2,1)S(1)} %combine.1.refs_0_, bf16[128,2048]{1,0:T(8,128)(2,1)S(1)} %collective-permute-done.5.refs_0_.refs_1_, ...), custom_call_target="tpu_custom_call" | custom-call | flops 4294967296 | bytes 8388608 | tf_op jit(solution)/shard_map/project/pallas_call | solution.py:422
  39.8 2.6 %collective-permute-start.10 = (bf16[32,2048]{1,0:T(8,128)(2,1)S(1)}, bf16[32,2048]{1,0:T(8,128)(2,1)S(1)}, u32[]{:S(2)}, u32[]{:S(2)}) collective-permute-start(bf16[32,2048]{1,0:T(8,128)(2,1)S(1)} %get-tuple-element.34), channel_id=1, source_target_pairs={{0,3},{1,2},{2,1},{3,0},{4,7},{5,6},{6,5},{7,4},{8,11},{9,10},{10,... | collective-permute-start | bytes 393224 | tf_op jit(solution)/shard_map/ppermute | solution.py:589
  42.3 0.7 %collective-permute-start.8 = (bf16[32,2048]{1,0:T(8,128)(2,1)S(1)}, bf16[32,2048]{1,0:T(8,128)(2,1)S(1)}, u32[]{:S(2)}, u32[]{:S(2)}) collective-permute-start(bf16[32,2048]{1,0:T(8,128)(2,1)S(1)} %get-tuple-element.32), channel_id=1, source_target_pairs={{0,1},{1,0},{2,3},{3,2},{4,5},{5,4},{6,7},{7,6},{8,9},{9,8},{10,11... | collective-permute-start | bytes 393224 | tf_op jit(solution)/shard_map/ppermute | solution.py:589
  43.0 1.2 %collective-permute-start.9 = (bf16[32,2048]{1,0:T(8,128)(2,1)S(1)}, bf16[32,2048]{1,0:T(8,128)(2,1)S(1)}, u32[]{:S(2)}, u32[]{:S(2)}) collective-permute-start(bf16[32,2048]{1,0:T(8,128)(2,1)S(1)} %get-tuple-element.33), channel_id=1, source_target_pairs={{0,2},{1,3},{2,0},{3,1},{4,6},{5,7},{6,4},{7,5},{8,10},{9,11},{10,... | collective-permute-start | bytes 393224 | tf_op jit(solution)/shard_map/ppermute | solution.py:589
  44.2 0.0 collective-permute-done.6.refs_1_
  44.3 4.4 %collective-permute-start.7 = (bf16[32,2048]{1,0:T(8,128)(2,1)S(1)}, bf16[32,2048]{1,0:T(8,128)(2,1)S(1)}, u32[]{:S(2)}, u32[]{:S(2)}) collective-permute-start(bf16[32,2048]{1,0:T(8,128)(2,1)S(1)} %add_convert_fusion), channel_id=1, source_target_pairs={{0,2},{1,3},{2,0},{3,1},{4,6},{5,7},{6,4},{7,5},{8,10},{9,11},{10,... | collective-permute-start | bytes 393224 | tf_op jit(solution)/shard_map/ppermute | solution.py:584
  48.7 0.5 collective-permute-done.10.refs_6_
  49.2 3.8 %collective-permute-done.8.refs_4_ = bf16[32,2048]{1,0:T(8,128)(2,1)S(1)} collective-permute-done((bf16[32,2048]{1,0:T(8,128)(2,1)S(1)}, bf16[32,2048]{1,0:T(8,128)(2,1)S(1)}, u32[]{:S(2)}, u32[]{:S(2)}) %collective-permute-start.8) | collective-permute-done | bytes 131104 | tf_op jit(solution)/shard_map/ppermute | solution.py:589
  53.1 4.9 %collective-permute-done.9.refs_5_ = bf16[32,2048]{1,0:T(8,128)(2,1)S(1)} collective-permute-done((bf16[32,2048]{1,0:T(8,128)(2,1)S(1)}, bf16[32,2048]{1,0:T(8,128)(2,1)S(1)}, u32[]{:S(2)}, u32[]{:S(2)}) %collective-permute-start.9) | collective-permute-done | bytes 131104 | tf_op jit(solution)/shard_map/ppermute | solution.py:589
  58.0 2.4 %collective-permute-done.7.refs_2_ = bf16[32,2048]{1,0:T(8,128)(2,1)S(1)} collective-permute-done((bf16[32,2048]{1,0:T(8,128)(2,1)S(1)}, bf16[32,2048]{1,0:T(8,128)(2,1)S(1)}, u32[]{:S(2)}, u32[]{:S(2)}) %collective-permute-start.7) | collective-permute-done | bytes 131104 | tf_op jit(solution)/shard_map/ppermute | solution.py:584
  60.3 0.8 %finish.1 = bf16[32,4096]{1,0:T(8,128)(2,1)} custom-call(f32[32,2048]{1,0:T(8,128)S(1)} %get-tuple-element.26.refs_0_, bf16[64,2048]{1,0:T(8,128)(2,1)S(1)} %collective-permute-done.6.refs_1_, bf16[32,2048]{1,0:T(8,128)(2,1)S(1)} %collective-permute-done.7.refs_2_, f32[32,2048]{1,0:T(8,128)S(1)} %get-tuple-element.31.refs_3_, ...), custom_call_target="tpu_custom_call" | custom-call | tf_op jit(solution)/shard_map/finish/pallas_call | solution.py:454
  (1 shorter events, 0.0 us)
Async XLA Ops:
  2.4 4.5 %collective-permute-start = (bf16[4672,128]{1,0:T(8,128)(2,1)S(1)}, bf16[4672,128]{1,0:T(8,128)(2,1)S(1)}, u32[]{:S(2)}, u32[]{:S(2)}) collective-permute-start(bf16[4672,128]{1,0:T(8,128)(2,1)S(1)} %pack.3), channel_id=1, source_target_pairs={{0,4},{4,0},{8,12},{12,8},{1,5},{5,1},{9,13},{13,9},{2,6},{6,2},{1... | collective-permute-start | bytes 3588104 | tf_op jit(solution)/shard_map/ppermute | solution.py:497
  2.9 12.7 %collective-permute-start.2 = (bf16[32,2048]{1,0:T(8,128)(2,1)S(1)}, bf16[32,2048]{1,0:T(8,128)(2,1)S(1)}, u32[]{:S(2)}, u32[]{:S(2)}) collective-permute-start(bf16[32,2048]{1,0:T(8,128)(2,1)S(1)} %get-tuple-element.20.refs_4_), channel_id=1, source_target_pairs={{0,12},{4,8},{8,4},{12,0},{1,13},{5,9},{9,5},{13,1},{2,14},{6,10},... | collective-permute-start | bytes 393224 | tf_op jit(solution)/shard_map/ppermute | solution.py:493
  5.6 10.1 %collective-permute-start.1 = (bf16[32,2048]{1,0:T(8,128)(2,1)S(1)}, bf16[32,2048]{1,0:T(8,128)(2,1)S(1)}, u32[]{:S(2)}, u32[]{:S(2)}) collective-permute-start(bf16[32,2048]{1,0:T(8,128)(2,1)S(1)} %get-tuple-element.21.rest_2_), channel_id=1, source_target_pairs={{0,8},{4,12},{8,0},{12,4},{1,9},{5,13},{9,1},{13,5},{2,10},{6,14},... | collective-permute-start | bytes 393224 | tf_op jit(solution)/shard_map/ppermute | solution.py:492
  13.6 17.0 %copy-start = (s32[128]{0:T(128)S(1)}, s32[128]{0:T(128)}, u32[]{:S(2)}) copy-start(s32[128]{0:T(128)} %dest_ref.1) | copy-start | bytes 1540
  13.6 8.9 %collective-permute-start.4 = (bf16[64,2176]{1,0:T(8,128)(2,1)S(1)}, bf16[64,2176]{1,0:T(8,128)(2,1)S(1)}, u32[]{:S(2)}, u32[]{:S(2)}) collective-permute-start(bf16[64,2176]{1,0:T(8,128)(2,1)S(1)} %get-tuple-element.22.a_ref), channel_id=1, source_target_pairs={{0,8},{4,12},{8,0},{12,4},{1,9},{5,13},{9,1},{13,5},{2,10},{6,14},... | collective-permute-start | bytes 835592 | tf_op jit(solution)/shard_map/ppermute | solution.py:534
  22.4 8.1 %collective-permute-start.3 = (bf16[64,2176]{1,0:T(8,128)(2,1)S(1)}, bf16[64,2176]{1,0:T(8,128)(2,1)S(1)}, u32[]{:S(2)}, u32[]{:S(2)}) collective-permute-start(bf16[64,2176]{1,0:T(8,128)(2,1)S(1)} %get-tuple-element.23.a_ref), channel_id=1, source_target_pairs={{0,8},{4,12},{8,0},{12,4},{1,9},{5,13},{9,1},{13,5},{2,10},{6,14},... | collective-permute-start | bytes 835592 | tf_op jit(solution)/shard_map/ppermute | solution.py:534
  31.3 2.0 %collective-permute-start.5 = (bf16[128,2048]{1,0:T(8,128)(2,1)S(1)}, bf16[128,2048]{1,0:T(8,128)(2,1)S(1)}, u32[]{:S(2)}, u32[]{:S(2)}) collective-permute-start(bf16[128,2048]{1,0:T(8,128)(2,1)S(1)} %combine.1.refs_0_), channel_id=1, source_target_pairs={{0,4},{4,0},{8,12},{12,8},{1,5},{5,1},{9,13},{13,9},{2,6},{6,2},{1... | collective-permute-start | bytes 1572872 | tf_op jit(solution)/shard_map/ppermute | solution.py:536
  35.2 9.1 %collective-permute-start.6 = (bf16[64,2048]{1,0:T(8,128)(2,1)S(1)}, bf16[64,2048]{1,0:T(8,128)(2,1)S(1)}, u32[]{:S(2)}, u32[]{:S(2)}) collective-permute-start(bf16[64,2048]{1,0:T(8,128)(2,1)S(1)} %get-tuple-element.27), channel_id=1, source_target_pairs={{0,1},{1,0},{2,3},{3,2},{4,5},{5,4},{6,7},{7,6},{8,9},{9,8},{10,11... | collective-permute-start | bytes 786440 | tf_op jit(solution)/shard_map/ppermute | solution.py:582
  39.8 9.5 %collective-permute-start.10 = (bf16[32,2048]{1,0:T(8,128)(2,1)S(1)}, bf16[32,2048]{1,0:T(8,128)(2,1)S(1)}, u32[]{:S(2)}, u32[]{:S(2)}) collective-permute-start(bf16[32,2048]{1,0:T(8,128)(2,1)S(1)} %get-tuple-element.34), channel_id=1, source_target_pairs={{0,3},{1,2},{2,1},{3,0},{4,7},{5,6},{6,5},{7,4},{8,11},{9,10},{10,... | collective-permute-start | bytes 393224 | tf_op jit(solution)/shard_map/ppermute | solution.py:589
  42.3 10.7 %collective-permute-start.8 = (bf16[32,2048]{1,0:T(8,128)(2,1)S(1)}, bf16[32,2048]{1,0:T(8,128)(2,1)S(1)}, u32[]{:S(2)}, u32[]{:S(2)}) collective-permute-start(bf16[32,2048]{1,0:T(8,128)(2,1)S(1)} %get-tuple-element.32), channel_id=1, source_target_pairs={{0,1},{1,0},{2,3},{3,2},{4,5},{5,4},{6,7},{7,6},{8,9},{9,8},{10,11... | collective-permute-start | bytes 393224 | tf_op jit(solution)/shard_map/ppermute | solution.py:589
  43.0 14.9 %collective-permute-start.9 = (bf16[32,2048]{1,0:T(8,128)(2,1)S(1)}, bf16[32,2048]{1,0:T(8,128)(2,1)S(1)}, u32[]{:S(2)}, u32[]{:S(2)}) collective-permute-start(bf16[32,2048]{1,0:T(8,128)(2,1)S(1)} %get-tuple-element.33), channel_id=1, source_target_pairs={{0,2},{1,3},{2,0},{3,1},{4,6},{5,7},{6,4},{7,5},{8,10},{9,11},{10,... | collective-permute-start | bytes 393224 | tf_op jit(solution)/shard_map/ppermute | solution.py:589
  44.3 16.0 %collective-permute-start.7 = (bf16[32,2048]{1,0:T(8,128)(2,1)S(1)}, bf16[32,2048]{1,0:T(8,128)(2,1)S(1)}, u32[]{:S(2)}, u32[]{:S(2)}) collective-permute-start(bf16[32,2048]{1,0:T(8,128)(2,1)S(1)} %add_convert_fusion), channel_id=1, source_target_pairs={{0,2},{1,3},{2,0},{3,1},{4,6},{5,7},{6,4},{7,5},{8,10},{9,11},{10,... | collective-permute-start | bytes 393224 | tf_op jit(solution)/shard_map/ppermute | solution.py:584

commit v3 on v2

--- a/solution.py
+++ b/solution.py
@@ -16,8 +16,8 @@
 NEG = -1e30
 SCALE = 1.0 / math.sqrt(HEAD_DIM)
 LOG2E = math.log2(math.e)
-SPANS = 2
-COPIES = 4
+SPANS = (2, 2, 2, 2)
+COPIES = 2
 
 
 def moves(*arrays):
@@ -34,9 +34,9 @@
     return lax.rem(lax.axis_index("ctx"), 2)
 
 
-def pack_kernel(number, kv, other, *refs):
+def pack_kernel(number, kv, *refs):
     sources, out_ref, sems = refs[:-2], refs[-2], refs[-1]
-    block = (1 - my_half() if other else my_half()) * kv + number
+    block = (1 - my_half()) * kv + number
     copies = []
     at = 0
     for ref in sources[:4]:
@@ -48,8 +48,8 @@
         rows = ref.shape[0]
         heads = (out_ref.shape[0] - at) // rows
         for g in range(heads):
-            first = (number * heads + g) * HEAD_DIM
-            copies.append((ref.at[:, first : first + HEAD_DIM], out_ref.at[at : at + rows, :]))
+            first = pl.multiple_of((block * heads + g) * HEAD_DIM, HEAD_DIM)
+            copies.append((ref.at[:, pl.ds(first, HEAD_DIM)], out_ref.at[at : at + rows, :]))
             at += rows
     copies = [pltpu.make_async_copy(a, b, sems.at[n]) for n, (a, b) in enumerate(copies)]
     for c in copies:
@@ -58,47 +58,54 @@
         c.wait()
 
 
-def pack(other, arrays, queries, kv, number):
-    group = queries[0].shape[1] // HEAD_DIM // kv if queries else 0
-    rows = sum(a.shape[0] for a in arrays) + sum(q.shape[0] * group for q in queries)
+def pack(arrays, queries, kv, number):
+    group = queries.shape[1] // arrays[0].shape[1]
+    rows = sum(a.shape[0] for a in arrays) + queries.shape[0] * group
     return pl.pallas_call(
-        functools.partial(pack_kernel, number, kv, other),
-        in_specs=[pl.BlockSpec(memory_space=pltpu.HBM)] * len(arrays)
-        + [pl.BlockSpec(memory_space=pltpu.VMEM)] * len(queries),
+        functools.partial(pack_kernel, number, kv),
+        in_specs=[pl.BlockSpec(memory_space=pltpu.HBM)] * (len(arrays) + 1),
         out_specs=pl.BlockSpec(memory_space=pltpu.VMEM),
         out_shape=jax.ShapeDtypeStruct((rows, HEAD_DIM), arrays[0].dtype),
         scratch_shapes=[pltpu.SemaphoreType.DMA((len(arrays) + group,))],
         compiler_params=pltpu.CompilerParams(vmem_limit_bytes=4 * 2**20),
         cost_estimate=moves(jax.ShapeDtypeStruct((rows, HEAD_DIM), arrays[0].dtype)),
         name="pack",
-    )(*[in_hbm(a) for a in arrays], *queries)
-
-
-def split_kernel(q_ref, *refs):
-    outs, sems = refs[:-1], refs[-1]
+    )(*[in_hbm(a) for a in (*arrays, queries)])
+
+
+def prepare_kernel(kv, *refs):
+    sources, q_ref, packed, outs, sems = refs[:4], refs[4], refs[5 : 5 + kv], refs[-3:-1], refs[-1]
+    copies = []
+    for i in range(kv):
+        at = 0
+        for ref in sources:
+            rows = ref.shape[0]
+            first = pl.multiple_of((my_half() * kv + i) * HEAD_DIM, HEAD_DIM)
+            copies.append((ref.at[:, pl.ds(first, HEAD_DIM)], packed[i].at[at : at + rows, :]))
+            at += rows
     width = outs[0].shape[1]
-    copies = []
     for n, out in enumerate(outs):
         columns = pl.ds(pl.multiple_of((my_half() ^ n) * width, width), width)
-        copies.append(pltpu.make_async_copy(q_ref.at[:, columns], out, sems.at[n]))
+        copies.append((q_ref.at[:, columns], out))
+    copies = [pltpu.make_async_copy(a, b, sems.at[n]) for n, (a, b) in enumerate(copies)]
     for c in copies:
         c.start()
     for c in copies:
         c.wait()
 
 
-def split(a):
-    half = jax.ShapeDtypeStruct((a.shape[0], a.shape[1] // 2), a.dtype)
+def prepare(arrays, queries, kv):
+    rows = sum(a.shape[0] for a in arrays)
+    half = jax.ShapeDtypeStruct((queries.shape[0], queries.shape[1] // 2), queries.dtype)
     return pl.pallas_call(
-        split_kernel,
-        in_specs=[pl.BlockSpec(memory_space=pltpu.HBM)],
-        out_specs=[pl.BlockSpec(memory_space=pltpu.VMEM)] * 2,
-        out_shape=[half, half],
-        scratch_shapes=[pltpu.SemaphoreType.DMA((2,))],
+        functools.partial(prepare_kernel, kv),
+        in_specs=[pl.BlockSpec(memory_space=pltpu.HBM)] * (len(arrays) + 1),
+        out_specs=[pl.BlockSpec(memory_space=pltpu.VMEM)] * (kv + 2),
+        out_shape=[jax.ShapeDtypeStruct((rows, HEAD_DIM), queries.dtype)] * kv + [half, half],
+        scratch_shapes=[pltpu.SemaphoreType.DMA((4 * kv + 2,))],
         compiler_params=pltpu.CompilerParams(vmem_limit_bytes=2 * 2**20),
-        cost_estimate=moves(a),
-        name="split",
-    )(in_hbm(a))
+        name="prepare",
+    )(*[in_hbm(a) for a in (*arrays, queries)])
 
 
 def attention_kernel(
@@ -110,19 +117,22 @@
     query_blocks = len(row_blocks)
     reqs = new_ref.shape[1]
     packed = rest[:shards]
-    q_refs = rest[shards : -4 - SPANS]
-    out_ref, held = rest[-4 - SPANS], rest[-3 - SPANS : -3]
+    spans = len(SPANS)
+    q_refs = rest[shards : -4 - spans]
+    out_ref, held = rest[-4 - spans], rest[-3 - spans : -3]
     sorted_q, part, sems = rest[-3:]
     copies = []
-    for j, there in enumerate(held):
+    column = 0
+    for there in held:
         rows, width = there.shape
         share = rows // COPIES
         for n in range(COPIES):
             first = pl.multiple_of(weight_block() * rows + n * share, ALIGN)
-            source = weight_ref.at[pl.ds(first, share), j * width : (j + 1) * width]
+            source = weight_ref.at[pl.ds(first, share), column : column + width]
             target = there.at[n * share : (n + 1) * share, :]
             copies.append(pltpu.make_async_copy(source, target, sems.at[len(copies)]))
             copies[-1].start()
+        column += width
     padded = sorted_q.shape[0]
     cols = sorted_q.shape[1]
     group = cols // HEAD_DIM
@@ -289,15 +299,15 @@
         in_specs=[pl.BlockSpec(memory_space=pltpu.SMEM)] * 2
         + [pl.BlockSpec(memory_space=pltpu.HBM)]
         + [vmem] * (sets + len(queries)),
-        out_specs=[vmem] * (1 + SPANS),
+        out_specs=[vmem] * (1 + len(SPANS)),
         scratch_shapes=[
             pltpu.VMEM((padded, cols), jnp.bfloat16),
             pltpu.VMEM((padded, cols + 128), jnp.bfloat16),
-            pltpu.SemaphoreType.DMA((SPANS * COPIES,)),
+            pltpu.SemaphoreType.DMA((len(SPANS) * COPIES,)),
         ],
         out_shape=[
             jax.ShapeDtypeStruct((all_rows, cols + 128), jnp.bfloat16),
-            *[pltpu.VMEM((cols, weight.shape[1] // SPANS), weight.dtype)] * SPANS,
+            *[pltpu.VMEM((cols, weight.shape[1] // 8 * n), weight.dtype) for n in SPANS],
         ],
         compiler_params=pltpu.CompilerParams(vmem_limit_bytes=8 * 2**20),
         cost_estimate=pl.CostEstimate(
@@ -488,13 +498,13 @@
         near = [(i, i ^ 1) for i in range(blocks)]
         far = [(i, i ^ 2) for i in range(blocks)]
         across = [(i, i ^ 3) for i in range(blocks)]
-        q_mine, q_other = split(queries)
+        *own_packed, q_mine, q_other = prepare(caches, queries, kv)
         q_far = lax.ppermute(q_mine, "ctx", far)
         q_across = lax.ppermute(q_other, "ctx", across)
         packed = [
             [
-                pack(False, caches, [], kv, i),
-                lax.ppermute(pack(True, caches, [q_other], kv, i), "ctx", near),
+                own_packed[i],
+                lax.ppermute(pack(caches, queries, kv, i), "ctx", near),
             ]
             for i in range(kv)
         ]
@@ -556,7 +566,7 @@
             )
 
     hops = [[(i, i ^ d if even else (i + d) % heads) for i in range(heads)] for d in range(heads)]
-    step = out_weight.shape[1] // SPANS // 4
+    step = out_weight.shape[1] // 8
     direct_cuts = [
         (d * out_rows, (d + 1) * out_rows, jnp.bfloat16 if d else jnp.float32) for d in range(heads)
     ]
@@ -566,11 +576,11 @@
         (2 * out_rows, 4 * out_rows, jnp.bfloat16),
     ]
     chunks = []
-    for number in range(SPANS):
+    for number in range(len(SPANS)):
         span = [w[number] for w in weights]
-        by_pairs = halving and number == 0
+        by_pairs = halving
         cuts = pair_cuts if by_pairs else direct_cuts
-        if others and number == 0:
+        if others and number == len(SPANS) - 1:
             whole = [(0, all_rows, jnp.float32)]
             begun = project(mine, span[:kv], whole, step)
             shares = project(others, span[kv:], cuts, step, begun)

time: 61.3 us -> 58.7 us (0.958)
  waiting for transfers between devices: 19.2 us -> 17.9 us
  Pallas kernels: 25.8 us -> 24.6 us
    ppermute x4 -> x1, waiting for transfers between devices: 9.26 us -> 0.01 us  [per_device(): lax.ppermute(pack(caches, queries, kv, i), 'ctx', near)]
    ppermute x4 -> x1, starting transfers between devices: 4.97 us -> 0.52 us  [per_device(): lax.ppermute(pack(caches, queries, kv, i), 'ctx', near)]
    ppermute x1 -> x4, waiting for transfers between devices: 2.36 us -> 5.99 us  [per_device(): chunks.append([shares[0], got, lax.ppermute(away, 'head', hops[2])])]
    ppermute x1 -> x4, waiting for transfers between devices: 0.01 us -> 3.18 us  [per_device(): got = lax.ppermute(shares[2], 'head', hops[1])]
    ppermute x1 -> x4, starting transfers between devices: 1.66 us -> 4.29 us  [per_device(): got = lax.ppermute(shares[2], 'head', hops[1])]
    ppermute x1, starting transfers between devices: 0.04 us -> 2.61 us  [per_device(): q_far = lax.ppermute(q_mine, 'ctx', far)]
    ppermute x1, starting transfers between devices: 2.64 us -> 0.16 us  [per_device(): q_across = lax.ppermute(q_other, 'ctx', across)]
    ppermute x1 -> x4, starting transfers between devices: 4.43 us -> 5.95 us  [per_device(): chunks.append([shares[0], got, lax.ppermute(away, 'head', hops[2])])]
  transfers between devices with their start and end apart: 11 -> 14, of which waited for: 6 -> 7; matrix products, arithmetic and copies ran while one was open for 0% -> 0% of each run, Pallas kernels for 33% -> 35%
where the time goes in v3:
time: 58.7 us; the launch traced here: 58.5 us
  Pallas kernels  24.6 us (42%)
  waiting for transfers between devices  17.9 us (30%)
  starting transfers between devices  15.8 us (27%)
    pallas_call x2, Pallas kernels, attend(): pl.pallas_call(functools.partial(attention_kernel, key_blocks, query_bloc...  13.6 us
    ppermute x1, waiting for transfers between devices, per_device(): lax.ppermute(other, 'ctx', far)  7.76 us
    pallas_call x5, Pallas kernels, project(): pl.pallas_call(functools.partial(project_kernel, len(parts), len(added),...  6.26 us
    ppermute x4, waiting for transfers between devices, per_device(): chunks.append([shares[0], got, lax.ppermute(away, 'head', hops[2])])  5.99 us
    ppermute x4, starting transfers between devices, per_device(): chunks.append([shares[0], got, lax.ppermute(away, 'head', hops[2])])  5.95 us
    ppermute x4, starting transfers between devices, per_device(): got = lax.ppermute(shares[2], 'head', hops[1])  4.29 us
    ppermute x4, waiting for transfers between devices, per_device(): got = lax.ppermute(shares[2], 'head', hops[1])  3.18 us
    ppermute x1, starting transfers between devices, per_device(): q_far = lax.ppermute(q_mine, 'ctx', far)  2.61 us
  transfers between devices with their start and end apart: 14, of which 7 were waited for; matrix products, arithmetic and copies ran while one was open for 0% of the time, Pallas kernels for 35%

profile of v3, /device:TPU:0, one launch (start us, length us, event | category | flops | bytes accessed | tf_op | source)
XLA Modules:
  0.0 58.5 jit_solution(4958903740075715895)
XLA Ops:
  0.0 1.4 %pack.1 = bf16[4672,128]{1,0:T(8,128)(2,1)S(1)} custom-call(bf16[2048,256]{1,0:T(8,128)(2,1)} %refs_0_.3, bf16[2048,256]{1,0:T(8,128)(2,1)} %refs_1_.3, bf16[32,256]{1,0:T(8,128)(2,1)} %refs_2_.3, bf16[32,256]{1,0:T(8,128)(2,1)} %refs_3_.3, bf16[32,4096]{1,0:T(8,128)(2,1)} %refs_4_.3), custom_call_target="tpu_custom_call" | custom-call | bytes 2392064 | tf_op jit(solution)/shard_map/pack/pallas_call | solution.py:64
  1.4 0.5 collective-permute-start
  1.9 1.3 %prepare.1 = (bf16[4160,128]{1,0:T(8,128)(2,1)S(1)}, bf16[32,2048]{1,0:T(8,128)(2,1)S(1)}, bf16[32,2048]{1,0:T(8,128)(2,1)S(1)}) custom-call(bf16[2048,256]{1,0:T(8,128)(2,1)} %refs_0_.3, bf16[2048,256]{1,0:T(8,128)(2,1)} %refs_1_.3, bf16[32,256]{1,0:T(8,128)(2,1)} %refs_2_.3, bf16[32,256]{1,0:T(8,128)(2,1)} %refs_3_.3, bf16[32,4096]{1,0:T(8,128)(2,1)} %refs_4_.3), custom_call_target="tpu_custom_call" | custom-call | tf_op jit(solution)/shard_map/prepare/pallas_call | solution.py:100
  3.3 2.6 %collective-permute-start.1 = (bf16[32,2048]{1,0:T(8,128)(2,1)S(1)}, bf16[32,2048]{1,0:T(8,128)(2,1)S(1)}, u32[]{:S(2)}, u32[]{:S(2)}) collective-permute-start(bf16[32,2048]{1,0:T(8,128)(2,1)S(1)} %get-tuple-element.31.rest_2_), channel_id=1, source_target_pairs={{0,8},{4,12},{8,0},{12,4},{1,9},{5,13},{9,1},{13,5},{2,10},{6,14},... | collective-permute-start | bytes 393224 | tf_op jit(solution)/shard_map/ppermute | solution.py:502
  5.9 0.2 collective-permute-start.2
  6.1 0.0 collective-permute-done.rest_1_
  6.1 6.8 %attend.2 = (bf16[64,2176]{1,0:T(8,128)(2,1)S(1)}, bf16[2048,1024]{1,0:T(8,128)(2,1)S(1)}, bf16[2048,1024]{1,0:T(8,128)(2,1)S(1)}, bf16[2048,1024]{1,0:T(8,128)(2,1)S(1)}, bf16[2048,1024]{1,0:T(8,128)(2,1)S(1)}) custom-call(s32[4,4]{1,0:T(4,128)} %new_ref.3, s32[4,4]{1,0:T(4,128)} %cache_ref.3, bf16[4096,4096]{1,0:T(8,128)(2,1)} %weight_ref.3, ...), custom_call_target="tpu_custom_call" | custom-call | flops 1937768448 | bytes 16777216 | tf_op jit(solution)/shard_map/attend/pallas_call | solution.py:294
  12.8 0.0 copy-start
  12.8 1.8 %collective-permute-start.4 = (bf16[64,2176]{1,0:T(8,128)(2,1)S(1)}, bf16[64,2176]{1,0:T(8,128)(2,1)S(1)}, u32[]{:S(2)}, u32[]{:S(2)}) collective-permute-start(bf16[64,2176]{1,0:T(8,128)(2,1)S(1)} %get-tuple-element.32.a_ref), channel_id=1, source_target_pairs={{0,8},{4,12},{8,0},{12,4},{1,9},{5,13},{9,1},{13,5},{2,10},{6,14},... | collective-permute-start | bytes 835592 | tf_op jit(solution)/shard_map/ppermute | solution.py:544
  14.6 0.0 collective-permute-done.1.rest_2_
  14.6 0.0 collective-permute-done.2.rest_3_
  14.6 6.8 %attend.3 = (bf16[64,2176]{1,0:T(8,128)(2,1)S(1)}, bf16[2048,1024]{1,0:T(8,128)(2,1)S(1)}, bf16[2048,1024]{1,0:T(8,128)(2,1)S(1)}, bf16[2048,1024]{1,0:T(8,128)(2,1)S(1)}, bf16[2048,1024]{1,0:T(8,128)(2,1)S(1)}) custom-call(s32[4,4]{1,0:T(4,128)} %new_ref.3, s32[4,4]{1,0:T(4,128)} %cache_ref.3, bf16[4096,4096]{1,0:T(8,128)(2,1)} %weight_ref.3, ...), custom_call_target="tpu_custom_call" | custom-call | flops 1937768448 | bytes 16777216 | tf_op jit(solution)/shard_map/attend/pallas_call | solution.py:294
  21.4 0.4 collective-permute-start.3
  21.8 0.0 collective-permute-done.4.b_ref
  21.8 0.5 mix.1.far_ref
  22.3 7.8 %collective-permute-done.3.b_ref = bf16[64,2176]{1,0:T(8,128)(2,1)S(1)} collective-permute-done((bf16[64,2176]{1,0:T(8,128)(2,1)S(1)}, bf16[64,2176]{1,0:T(8,128)(2,1)S(1)}, u32[]{:S(2)}, u32[]{:S(2)}) %collective-permute-start.3) | collective-permute-done | bytes 278560 | tf_op jit(solution)/shard_map/ppermute | solution.py:544
  30.1 0.0 copy-done
  30.1 0.8 %combine.1.refs_0_ = bf16[128,2048]{1,0:T(8,128)(2,1)S(1)} custom-call(s32[128]{0:T(128)S(1)} %copy-done, bf16[64,2176]{1,0:T(8,128)(2,1)S(1)} %get-tuple-element.32.a_ref, bf16[64,2176]{1,0:T(8,128)(2,1)S(1)} %collective-permute-done.3.b_ref, bf16[64,2048]{1,0:T(8,128)(2,1)S(1)} %mix.1.far_ref), custom_call_target="tpu_custom_call" | custom-call | bytes 1638400 | tf_op jit(solution)/shard_map/combine/pallas_call | solution.py:399
  30.8 0.1 collective-permute-start.5
  30.9 0.9 %project.8.refs_2_ = f32[128,1024]{1,0:T(8,128)S(1)} custom-call(bf16[128,2048]{1,0:T(8,128)(2,1)S(1)} %combine.1.refs_0_, bf16[2048,1024]{1,0:T(8,128)(2,1)S(1)} %get-tuple-element.51.refs_1_), custom_call_target="tpu_custom_call" | custom-call | flops 1073741824 | bytes 2097152 | tf_op jit(solution)/shard_map/project/pallas_call | solution.py:432
  31.8 1.0 %collective-permute-done.5.refs_1_.refs_0_ = bf16[128,2048]{1,0:T(8,128)(2,1)S(1)} collective-permute-done((bf16[128,2048]{1,0:T(8,128)(2,1)S(1)}, bf16[128,2048]{1,0:T(8,128)(2,1)S(1)}, u32[]{:S(2)}, u32[]{:S(2)}) %collective-permute-start.5) | collective-permute-done | bytes 524320 | tf_op jit(solution)/shard_map/ppermute | solution.py:546
  32.8 0.9 %project.9 = (f32[32,1024]{1,0:T(8,128)S(1)}, f32[32,1024]{1,0:T(8,128)S(1)}, bf16[64,1024]{1,0:T(8,128)(2,1)S(1)}) custom-call(bf16[128,2048]{1,0:T(8,128)(2,1)S(1)} %collective-permute-done.5.refs_1_.refs_0_, bf16[2048,1024]{1,0:T(8,128)(2,1)S(1)} %get-tuple-element.50.refs_1_, f32[128,1024]{1,0:T(8,128)S(1)} %project.8.refs_2_), custom_call_target="tpu_custom_call" | custom-call | flops 1073741824 | bytes 2097152 | tf_op jit(solution)/shard_map/project/pallas_call | solution.py:432
  33.7 1.6 %collective-permute-start.12 = (bf16[64,1024]{1,0:T(8,128)(2,1)S(1)}, bf16[64,1024]{1,0:T(8,128)(2,1)S(1)}, u32[]{:S(2)}, u32[]{:S(2)}) collective-permute-start(bf16[64,1024]{1,0:T(8,128)(2,1)S(1)} %get-tuple-element.53), channel_id=1, source_target_pairs={{0,1},{1,0},{2,3},{3,2},{4,5},{5,4},{6,7},{7,6},{8,9},{9,8},{10,11... | collective-permute-start | bytes 393224 | tf_op jit(solution)/shard_map/ppermute | solution.py:592
  35.4 1.5 %project.7 = (f32[32,1024]{1,0:T(8,128)S(1)}, f32[32,1024]{1,0:T(8,128)S(1)}, bf16[64,1024]{1,0:T(8,128)(2,1)S(1)}) custom-call(bf16[128,2048]{1,0:T(8,128)(2,1)S(1)} %combine.1.refs_0_, bf16[128,2048]{1,0:T(8,128)(2,1)S(1)} %collective-permute-done.5.refs_1_.refs_0_, bf16[2048,1024]{1,0:T(8,128)(2,1)S(1)} %get-tuple-element.45.refs_2_, ...), custom_call_target="tpu_custom_call" | custom-call | flops 2147483648 | bytes 4194304 | tf_op jit(solution)/shard_map/project/pallas_call | solution.py:432
  36.9 0.5 collective-permute-start.10
  37.4 1.5 %project.6 = (f32[32,1024]{1,0:T(8,128)S(1)}, f32[32,1024]{1,0:T(8,128)S(1)}, bf16[64,1024]{1,0:T(8,128)(2,1)S(1)}) custom-call(bf16[128,2048]{1,0:T(8,128)(2,1)S(1)} %combine.1.refs_0_, bf16[128,2048]{1,0:T(8,128)(2,1)S(1)} %collective-permute-done.5.refs_1_.refs_0_, bf16[2048,1024]{1,0:T(8,128)(2,1)S(1)} %get-tuple-element.40.refs_2_, ...), custom_call_target="tpu_custom_call" | custom-call | flops 2147483648 | bytes 4194304 | tf_op jit(solution)/shard_map/project/pallas_call | solution.py:432
  38.8 1.6 %collective-permute-start.8 = (bf16[64,1024]{1,0:T(8,128)(2,1)S(1)}, bf16[64,1024]{1,0:T(8,128)(2,1)S(1)}, u32[]{:S(2)}, u32[]{:S(2)}) collective-permute-start(bf16[64,1024]{1,0:T(8,128)(2,1)S(1)} %get-tuple-element.43), channel_id=1, source_target_pairs={{0,1},{1,0},{2,3},{3,2},{4,5},{5,4},{6,7},{7,6},{8,9},{9,8},{10,11... | collective-permute-start | bytes 393224 | tf_op jit(solution)/shard_map/ppermute | solution.py:592
  40.5 1.5 %project.5 = (f32[32,1024]{1,0:T(8,128)S(1)}, f32[32,1024]{1,0:T(8,128)S(1)}, bf16[64,1024]{1,0:T(8,128)(2,1)S(1)}) custom-call(bf16[128,2048]{1,0:T(8,128)(2,1)S(1)} %combine.1.refs_0_, bf16[128,2048]{1,0:T(8,128)(2,1)S(1)} %collective-permute-done.5.refs_1_.refs_0_, bf16[2048,1024]{1,0:T(8,128)(2,1)S(1)} %get-tuple-element.35.refs_2_, ...), custom_call_target="tpu_custom_call" | custom-call | flops 2147483648 | bytes 4194304 | tf_op jit(solution)/shard_map/project/pallas_call | solution.py:432
  42.0 0.5 collective-permute-start.6
  42.5 0.0 collective-permute-done.12.refs_10_
  42.5 2.7 %collective-permute-start.13 = (bf16[32,1024]{1,0:T(8,128)(2,1)S(1)}, bf16[32,1024]{1,0:T(8,128)(2,1)S(1)}, u32[]{:S(2)}, u32[]{:S(2)}) collective-permute-start(bf16[32,1024]{1,0:T(8,128)(2,1)S(1)} %add_convert_fusion), channel_id=1, source_target_pairs={{0,2},{1,3},{2,0},{3,1},{4,6},{5,7},{6,4},{7,5},{8,10},{9,11},{10,... | collective-permute-start | bytes 196616 | tf_op jit(solution)/shard_map/ppermute | solution.py:594
  45.2 0.0 collective-permute-done.10.refs_7_
  45.2 0.8 %collective-permute-start.11 = (bf16[32,1024]{1,0:T(8,128)(2,1)S(1)}, bf16[32,1024]{1,0:T(8,128)(2,1)S(1)}, u32[]{:S(2)}, u32[]{:S(2)}) collective-permute-start(bf16[32,1024]{1,0:T(8,128)(2,1)S(1)} %add_convert_fusion.1), channel_id=1, source_target_pairs={{0,2},{1,3},{2,0},{3,1},{4,6},{5,7},{6,4},{7,5},{8,10},{9,11},{10,... | collective-permute-start | bytes 196616 | tf_op jit(solution)/shard_map/ppermute | solution.py:594
  45.9 0.7 %collective-permute-done.8.refs_4_ = bf16[64,1024]{1,0:T(8,128)(2,1)S(1)} collective-permute-done((bf16[64,1024]{1,0:T(8,128)(2,1)S(1)}, bf16[64,1024]{1,0:T(8,128)(2,1)S(1)}, u32[]{:S(2)}, u32[]{:S(2)}) %collective-permute-start.8) | collective-permute-done | bytes 131104 | tf_op jit(solution)/shard_map/ppermute | solution.py:592
  46.7 2.1 %collective-permute-start.9 = (bf16[32,1024]{1,0:T(8,128)(2,1)S(1)}, bf16[32,1024]{1,0:T(8,128)(2,1)S(1)}, u32[]{:S(2)}, u32[]{:S(2)}) collective-permute-start(bf16[32,1024]{1,0:T(8,128)(2,1)S(1)} %add_convert_fusion.2), channel_id=1, source_target_pairs={{0,2},{1,3},{2,0},{3,1},{4,6},{5,7},{6,4},{7,5},{8,10},{9,11},{10,... | collective-permute-start | bytes 196616 | tf_op jit(solution)/shard_map/ppermute | solution.py:594
  48.8 2.4 %collective-permute-done.6.refs_1_ = bf16[64,1024]{1,0:T(8,128)(2,1)S(1)} collective-permute-done((bf16[64,1024]{1,0:T(8,128)(2,1)S(1)}, bf16[64,1024]{1,0:T(8,128)(2,1)S(1)}, u32[]{:S(2)}, u32[]{:S(2)}) %collective-permute-start.6) | collective-permute-done | bytes 131104 | tf_op jit(solution)/shard_map/ppermute | solution.py:592
  51.3 0.4 collective-permute-start.7
  51.7 0.0 collective-permute-done.13.refs_11_
  51.7 3.2 %collective-permute-done.11.refs_8_ = bf16[32,1024]{1,0:T(8,128)(2,1)S(1)} collective-permute-done((bf16[32,1024]{1,0:T(8,128)(2,1)S(1)}, bf16[32,1024]{1,0:T(8,128)(2,1)S(1)}, u32[]{:S(2)}, u32[]{:S(2)}) %collective-permute-start.11) | collective-permute-done | bytes 65568 | tf_op jit(solution)/shard_map/ppermute | solution.py:594
  54.9 2.1 %collective-permute-done.9.refs_5_ = bf16[32,1024]{1,0:T(8,128)(2,1)S(1)} collective-permute-done((bf16[32,1024]{1,0:T(8,128)(2,1)S(1)}, bf16[32,1024]{1,0:T(8,128)(2,1)S(1)}, u32[]{:S(2)}, u32[]{:S(2)}) %collective-permute-start.9) | collective-permute-done | bytes 65568 | tf_op jit(solution)/shard_map/ppermute | solution.py:594
  57.0 0.7 %collective-permute-done.7.refs_2_ = bf16[32,1024]{1,0:T(8,128)(2,1)S(1)} collective-permute-done((bf16[32,1024]{1,0:T(8,128)(2,1)S(1)}, bf16[32,1024]{1,0:T(8,128)(2,1)S(1)}, u32[]{:S(2)}, u32[]{:S(2)}) %collective-permute-start.7) | collective-permute-done | bytes 65568 | tf_op jit(solution)/shard_map/ppermute | solution.py:594
  57.7 0.8 %finish.1 = bf16[32,4096]{1,0:T(8,128)(2,1)} custom-call(f32[32,1024]{1,0:T(8,128)S(1)} %get-tuple-element.37.refs_0_, bf16[64,1024]{1,0:T(8,128)(2,1)S(1)} %collective-permute-done.6.refs_1_, bf16[32,1024]{1,0:T(8,128)(2,1)S(1)} %collective-permute-done.7.refs_2_, f32[32,1024]{1,0:T(8,128)S(1)} %get-tuple-element.42.refs_3_, ...), custom_call_target="tpu_custom_call" | custom-call | tf_op jit(solution)/shard_map/finish/pallas_call | solution.py:464
  (4 shorter events, 0.1 us)
Async XLA Ops:
  1.4 4.6 %collective-permute-start = (bf16[4672,128]{1,0:T(8,128)(2,1)S(1)}, bf16[4672,128]{1,0:T(8,128)(2,1)S(1)}, u32[]{:S(2)}, u32[]{:S(2)}) collective-permute-start(bf16[4672,128]{1,0:T(8,128)(2,1)S(1)} %pack.1), channel_id=1, source_target_pairs={{0,4},{4,0},{8,12},{12,8},{1,5},{5,1},{9,13},{13,9},{2,6},{6,2},{1... | collective-permute-start | bytes 3588104 | tf_op jit(solution)/shard_map/ppermute | solution.py:507
  3.3 11.3 %collective-permute-start.1 = (bf16[32,2048]{1,0:T(8,128)(2,1)S(1)}, bf16[32,2048]{1,0:T(8,128)(2,1)S(1)}, u32[]{:S(2)}, u32[]{:S(2)}) collective-permute-start(bf16[32,2048]{1,0:T(8,128)(2,1)S(1)} %get-tuple-element.31.rest_2_), channel_id=1, source_target_pairs={{0,8},{4,12},{8,0},{12,4},{1,9},{5,13},{9,1},{13,5},{2,10},{6,14},... | collective-permute-start | bytes 393224 | tf_op jit(solution)/shard_map/ppermute | solution.py:502
  5.9 8.7 %collective-permute-start.2 = (bf16[32,2048]{1,0:T(8,128)(2,1)S(1)}, bf16[32,2048]{1,0:T(8,128)(2,1)S(1)}, u32[]{:S(2)}, u32[]{:S(2)}) collective-permute-start(bf16[32,2048]{1,0:T(8,128)(2,1)S(1)} %get-tuple-element.33), channel_id=1, source_target_pairs={{0,12},{4,8},{8,4},{12,0},{1,13},{5,9},{9,5},{13,1},{2,14},{6,10},... | collective-permute-start | bytes 393224 | tf_op jit(solution)/shard_map/ppermute | solution.py:503
  12.8 17.2 %copy-start = (s32[128]{0:T(128)S(1)}, s32[128]{0:T(128)}, u32[]{:S(2)}) copy-start(s32[128]{0:T(128)} %dest_ref.1) | copy-start | bytes 1540
  12.8 9.0 %collective-permute-start.4 = (bf16[64,2176]{1,0:T(8,128)(2,1)S(1)}, bf16[64,2176]{1,0:T(8,128)(2,1)S(1)}, u32[]{:S(2)}, u32[]{:S(2)}) collective-permute-start(bf16[64,2176]{1,0:T(8,128)(2,1)S(1)} %get-tuple-element.32.a_ref), channel_id=1, source_target_pairs={{0,8},{4,12},{8,0},{12,4},{1,9},{5,13},{9,1},{13,5},{2,10},{6,14},... | collective-permute-start | bytes 835592 | tf_op jit(solution)/shard_map/ppermute | solution.py:544
  21.4 8.6 %collective-permute-start.3 = (bf16[64,2176]{1,0:T(8,128)(2,1)S(1)}, bf16[64,2176]{1,0:T(8,128)(2,1)S(1)}, u32[]{:S(2)}, u32[]{:S(2)}) collective-permute-start(bf16[64,2176]{1,0:T(8,128)(2,1)S(1)} %get-tuple-element.34.a_ref), channel_id=1, source_target_pairs={{0,8},{4,12},{8,0},{12,4},{1,9},{5,13},{9,1},{13,5},{2,10},{6,14},... | collective-permute-start | bytes 835592 | tf_op jit(solution)/shard_map/ppermute | solution.py:544
  30.8 2.0 %collective-permute-start.5 = (bf16[128,2048]{1,0:T(8,128)(2,1)S(1)}, bf16[128,2048]{1,0:T(8,128)(2,1)S(1)}, u32[]{:S(2)}, u32[]{:S(2)}) collective-permute-start(bf16[128,2048]{1,0:T(8,128)(2,1)S(1)} %combine.1.refs_0_), channel_id=1, source_target_pairs={{0,4},{4,0},{8,12},{12,8},{1,5},{5,1},{9,13},{13,9},{2,6},{6,2},{1... | collective-permute-start | bytes 1572872 | tf_op jit(solution)/shard_map/ppermute | solution.py:546
  33.7 8.7 %collective-permute-start.12 = (bf16[64,1024]{1,0:T(8,128)(2,1)S(1)}, bf16[64,1024]{1,0:T(8,128)(2,1)S(1)}, u32[]{:S(2)}, u32[]{:S(2)}) collective-permute-start(bf16[64,1024]{1,0:T(8,128)(2,1)S(1)} %get-tuple-element.53), channel_id=1, source_target_pairs={{0,1},{1,0},{2,3},{3,2},{4,5},{5,4},{6,7},{7,6},{8,9},{9,8},{10,11... | collective-permute-start | bytes 393224 | tf_op jit(solution)/shard_map/ppermute | solution.py:592
  36.9 8.3 %collective-permute-start.10 = (bf16[64,1024]{1,0:T(8,128)(2,1)S(1)}, bf16[64,1024]{1,0:T(8,128)(2,1)S(1)}, u32[]{:S(2)}, u32[]{:S(2)}) collective-permute-start(bf16[64,1024]{1,0:T(8,128)(2,1)S(1)} %get-tuple-element.48), channel_id=1, source_target_pairs={{0,1},{1,0},{2,3},{3,2},{4,5},{5,4},{6,7},{7,6},{8,9},{9,8},{10,11... | collective-permute-start | bytes 393224 | tf_op jit(solution)/shard_map/ppermute | solution.py:592
  38.8 7.8 %collective-permute-start.8 = (bf16[64,1024]{1,0:T(8,128)(2,1)S(1)}, bf16[64,1024]{1,0:T(8,128)(2,1)S(1)}, u32[]{:S(2)}, u32[]{:S(2)}) collective-permute-start(bf16[64,1024]{1,0:T(8,128)(2,1)S(1)} %get-tuple-element.43), channel_id=1, source_target_pairs={{0,1},{1,0},{2,3},{3,2},{4,5},{5,4},{6,7},{7,6},{8,9},{9,8},{10,11... | collective-permute-start | bytes 393224 | tf_op jit(solution)/shard_map/ppermute | solution.py:592
  42.0 9.3 %collective-permute-start.6 = (bf16[64,1024]{1,0:T(8,128)(2,1)S(1)}, bf16[64,1024]{1,0:T(8,128)(2,1)S(1)}, u32[]{:S(2)}, u32[]{:S(2)}) collective-permute-start(bf16[64,1024]{1,0:T(8,128)(2,1)S(1)} %get-tuple-element.38), channel_id=1, source_target_pairs={{0,1},{1,0},{2,3},{3,2},{4,5},{5,4},{6,7},{7,6},{8,9},{9,8},{10,11... | collective-permute-start | bytes 393224 | tf_op jit(solution)/shard_map/ppermute | solution.py:592
  42.5 9.2 %collective-permute-start.13 = (bf16[32,1024]{1,0:T(8,128)(2,1)S(1)}, bf16[32,1024]{1,0:T(8,128)(2,1)S(1)}, u32[]{:S(2)}, u32[]{:S(2)}) collective-permute-start(bf16[32,1024]{1,0:T(8,128)(2,1)S(1)} %add_convert_fusion), channel_id=1, source_target_pairs={{0,2},{1,3},{2,0},{3,1},{4,6},{5,7},{6,4},{7,5},{8,10},{9,11},{10,... | collective-permute-start | bytes 196616 | tf_op jit(solution)/shard_map/ppermute | solution.py:594
  45.2 9.7 %collective-permute-start.11 = (bf16[32,1024]{1,0:T(8,128)(2,1)S(1)}, bf16[32,1024]{1,0:T(8,128)(2,1)S(1)}, u32[]{:S(2)}, u32[]{:S(2)}) collective-permute-start(bf16[32,1024]{1,0:T(8,128)(2,1)S(1)} %add_convert_fusion.1), channel_id=1, source_target_pairs={{0,2},{1,3},{2,0},{3,1},{4,6},{5,7},{6,4},{7,5},{8,10},{9,11},{10,... | collective-permute-start | bytes 196616 | tf_op jit(solution)/shard_map/ppermute | solution.py:594
  46.7 10.3 %collective-permute-start.9 = (bf16[32,1024]{1,0:T(8,128)(2,1)S(1)}, bf16[32,1024]{1,0:T(8,128)(2,1)S(1)}, u32[]{:S(2)}, u32[]{:S(2)}) collective-permute-start(bf16[32,1024]{1,0:T(8,128)(2,1)S(1)} %add_convert_fusion.2), channel_id=1, source_target_pairs={{0,2},{1,3},{2,0},{3,1},{4,6},{5,7},{6,4},{7,5},{8,10},{9,11},{10,... | collective-permute-start | bytes 196616 | tf_op jit(solution)/shard_map/ppermute | solution.py:594
  51.3 6.4 %collective-permute-start.7 = (bf16[32,1024]{1,0:T(8,128)(2,1)S(1)}, bf16[32,1024]{1,0:T(8,128)(2,1)S(1)}, u32[]{:S(2)}, u32[]{:S(2)}) collective-permute-start(bf16[32,1024]{1,0:T(8,128)(2,1)S(1)} %add_convert_fusion.3), channel_id=1, source_target_pairs={{0,2},{1,3},{2,0},{3,1},{4,6},{5,7},{6,4},{7,5},{8,10},{9,11},{10,... | collective-permute-start | bytes 196616 | tf_op jit(solution)/shard_map/ppermute | solution.py:594
